TPU v7x, 128 devices: a whole 4x4x4 slice. The times are simulated.
128 devices in a mesh: layer: 4 (over y), row: 4 (over x_hi, core), col: 8 (over x_lo, z).
Axes of the slice: x: 4 (x_hi: 2, x_lo: 2; x = x_hi * 2 + x_lo), y: 4, z: 4, core: 2. Of those that a mesh axis runs over, the one named last changes fastest.
Arguments:
- t2_slab: bfloat16 [16384, 4096], P('row', ('layer', 'col')), may hold values from -0.1875 to 0.1875
- lambda_block: bfloat16 [4096, 16384], P(('layer', 'row'), 'col'), may hold values from -6 to 6
Outputs:
- density_panel: bfloat16 [16384, 16384], P(('row', 'layer'), 'col')
All inputs are finite; a program needn't handle non-finite values.
Results may differ from a plain program's by a relative error of at most 0.015.
Values may be sent and summed in bfloat16 or wider, within the bound.
No kernel may reach another device: no remote copies, remote signals or barrier semaphores. Data moves between devices by JAX's collectives and lax.ppermute only.
A program may use at most 128 MiB of HBM per device.

v0:
```python
import jax
import jax.numpy as jnp
from jax import lax
from jax.sharding import PartitionSpec as P


def local(t2_slab, lambda_block):
    amplitude = lax.all_gather(t2_slab, "col", axis=1, tiled=True)
    lambda_layer = lax.all_gather(lambda_block, "row", axis=0, tiled=True)
    return lax.psum_scatter(
        jnp.dot(amplitude, lambda_layer, preferred_element_type=jnp.float32).astype(jnp.bfloat16),
        "layer",
        scatter_dimension=0,
        tiled=True,
    )


def solution(mesh):
    placed = (P("row", ("layer", "col")), P(("layer", "row"), "col"))
    return jax.shard_map(
        local, mesh=mesh, in_specs=placed, out_specs=P(("row", "layer"), "col"), check_vma=False
    )
```

profile of v0, /device:TPU:1, one launch (start us, length us, event | category | flops | bytes accessed | tf_op | source)
XLA Modules:
  0.0 329.3 jit_solution(1834171002844493062)
XLA Ops:
  6.5 0.0 all-gather.5.cloned.1.call-start
  6.5 0.7 all-gather.5.cloned.1.call-update
  7.3 0.0 all-gather.3.cloned.1.call-start
  7.3 0.7 all-gather.3.cloned.1.call-update
  8.0 0.0 reduce-scatter.2.cloned.1.call-start
  8.1 43.1 %all-gather.5.cloned.1.call-done = bf16[1024,2048]{1,0:T(8,128)(2,1)} async-done(((bf16[256,2048]{1,0:T(8,128)(2,1)}), bf16[1024,2048]{1,0:T(8,128)(2,1)}) %all-gather.5.cloned.1.call-update) | async-done | bytes 4194320 | tf_op jit(solution)/shard_map/all_gather | solution.py:9
  51.2 96.0 %all-gather.3.cloned.1.call-done = bf16[4096,1024]{1,0:T(8,128)(2,1)} async-done(((bf16[4096,128]{1,0:T(8,128)(2,1)}), bf16[4096,1024]{1,0:T(8,128)(2,1)}) %all-gather.3.cloned.1.call-update) | async-done | bytes 8388624 | tf_op jit(solution)/shard_map/all_gather | solution.py:8
  147.2 23.5 %convolution_convert_fusion = bf16[4096,2048]{1,0:T(8,128)(2,1)} fusion(bf16[4096,1024]{1,0:T(8,128)(2,1)} %all-gather.3.cloned.1.call-done, bf16[1024,2048]{1,0:T(8,128)(2,1)} %all-gather.5.cloned.1.call-done), kind=kOutput, calls=%fused_computation | convolution fusion | flops 17188257792 | bytes 29360128 | tf_op jit(solution)/shard_map/dot_general | solution.py:11
  170.7 0.0 reduce-scatter.2.cloned.1.call-update
  170.7 152.0 %reduce-scatter.2.cloned.1.call-done = bf16[1024,2048]{1,0:T(8,128)(2,1)} async-done(((bf16[4096,2048]{1,0:T(8,128)(2,1)}), bf16[1024,2048]{1,0:T(8,128)(2,1)}) %reduce-scatter.2.cloned.1.call-update) | async-done | bytes 4194320 | tf_op jit(solution)/shard_map/reduce_scatter | solution.py:10
Async XLA Ops:
  6.5 44.6 %all-gather.5.cloned.1.call-start = ((), (), s32[]{:S(2)}) async-start(), calls=%async_computation.2 | async-start | bytes 5242880 | tf_op jit(solution)/shard_map/all_gather | solution.py:9
  7.3 139.9 %all-gather.3.cloned.1.call-start = ((), (), s32[]{:S(2)}) async-start(), calls=%async_computation.1 | async-start | bytes 9437184 | tf_op jit(solution)/shard_map/all_gather | solution.py:8
  8.0 314.7 %reduce-scatter.2.cloned.1.call-start = ((), (), s32[]{:S(2)}) async-start(), calls=%async_computation.3 | async-start | bytes 20971520 | tf_op jit(solution)/shard_map/reduce_scatter | solution.py:10
Sparse Core Ops, SparseCore 0:
  9.0 42.1 all-gather.4
  52.8 94.4 all-gather.2
  170.8 151.8 reduce-scatter.1
where the time goes:
time: 329 us
  waiting for transfers between devices  293 us (89%)
  matrix products  23.5 us (7%)
  between operations  13.1 us (4%)
    reduce_scatter x1, waiting for transfers between devices, local(): lax.psum_scatter(jnp.dot(amplitude, lambda_layer, preferred_element_type=...  152 us
    all_gather x1, waiting for transfers between devices, local(): amplitude = lax.all_gather(t2_slab, 'col', axis=1, tiled=True)  96 us
    all_gather x1, waiting for transfers between devices, local(): lambda_layer = lax.all_gather(lambda_block, 'row', axis=0, tiled=True)  43.1 us
    dot_general x1, matrix products, local(): jnp.dot(amplitude, lambda_layer, preferred_element_type=jnp.float32)  23.5 us
  transfers between devices with their start and end apart: 3, of which 3 were waited for; matrix products, arithmetic and copies ran while one was open for 0% of the time, Pallas kernels for 0%

commit v1 on v0

v1 whole, which is shorter than its diff:
```python
import functools

import jax
import jax.numpy as jnp
from jax import lax
from jax.experimental import pallas as pl
from jax.experimental.pallas import tpu as pltpu
from jax.sharding import PartitionSpec as P

AXES = ("layer", "row", "col")
TILE = 256


def flat(y, xh, c, xl, z):
    return (y % 4 * 4 + xh % 2 * 2 + c % 2) * 8 + xl % 2 * 4 + z % 4


def pairs(move):
    return [
        (flat(y, xh, c, xl, z), flat(*move(y, xh, c, xl, z)))
        for y in range(4) for xh in range(2) for c in range(2) for xl in range(2) for z in range(4)
    ]


def way(c):
    return 1 if c == 0 else -1


Y_RING = pairs(lambda y, xh, c, xl, z: (y + way(c), xh, c, xl, z))
Y_BACK = pairs(lambda y, xh, c, xl, z: (y - way(c), xh, c, xl, z))
Y_FAR = pairs(lambda y, xh, c, xl, z: (y + 2, xh, c, xl, z))
Z_RING = pairs(lambda y, xh, c, xl, z: (y, xh, c, xl, z + way(c)))
XH = pairs(lambda y, xh, c, xl, z: (y, xh + 1, c, xl, z))
XL = pairs(lambda y, xh, c, xl, z: (y, xh, c, xl + 1, z))
CORE = pairs(lambda y, xh, c, xl, z: (y, xh, c + 1, xl, z))


def send(x, perm):
    return lax.ppermute(x, AXES, perm)


def multiply_kernel(places, n_a, n_b, has_acc, place_ref, *refs):
    a_refs, b_refs = refs[:n_a], refs[n_a : n_a + n_b]
    refs = refs[n_a + n_b :]
    acc_ref = refs[0] if has_acc else None
    out_ref, lhs, rhs, sems = refs[has_acc:]

    @pl.when(pl.program_id(0) == 0)
    def _():
        copies = []
        for i, (array, part) in enumerate(places):
            to = pl.ds(pl.multiple_of(place_ref[i] * 128, 128), 128)
            copies.append(pltpu.make_async_copy(a_refs[array].at[part], lhs.at[:, to], sems.at[i]))
        for i in range(n_b):
            to = pl.ds(pl.multiple_of(place_ref[len(places) + i] * 256, 256), 256)
            copies.append(pltpu.make_async_copy(b_refs[i], rhs.at[to], sems.at[len(places) + i]))
        for copy in copies:
            copy.start()
        for copy in copies:
            copy.wait()

    columns = pl.ds(pl.multiple_of(pl.program_id(0) * TILE, TILE), TILE)
    total = jnp.dot(lhs[:, :1024], rhs[:, columns], preferred_element_type=jnp.float32)
    if has_acc:
        total += acc_ref[...]
    out_ref[...] = total.astype(out_ref.dtype)


def multiply(acc, pieces, a_places, b_pieces, b_places, dtype):
    arrays, places = [], []
    for array, part in pieces:
        at = next((i for i, other in enumerate(arrays) if other is array), None)
        if at is None:
            at = len(arrays)
            arrays.append(array)
        places.append((at, part))
    n_a, n_b, has_acc = len(arrays), len(b_pieces), int(acc is not None)
    anywhere = pl.BlockSpec(memory_space=pl.ANY)
    tile = pl.BlockSpec((1024, TILE), lambda j, *_: (0, j))
    kernel = functools.partial(multiply_kernel, tuple(places), n_a, n_b, has_acc)
    return pl.pallas_call(
        kernel,
        grid_spec=pltpu.PrefetchScalarGridSpec(
            num_scalar_prefetch=1,
            grid=(2048 // TILE,),
            in_specs=[anywhere] * (n_a + n_b) + [tile] * has_acc,
            out_specs=tile,
            scratch_shapes=[
                pltpu.VMEM((1024, 2048), jnp.bfloat16),
                pltpu.VMEM((1024, 2048), jnp.bfloat16),
                pltpu.SemaphoreType.DMA((len(places) + n_b,)),
            ],
        ),
        out_shape=jax.ShapeDtypeStruct((1024, 2048), dtype),
        compiler_params=pltpu.CompilerParams(vmem_limit_bytes=32 * 2**20),
        cost_estimate=pl.CostEstimate(flops=2 * 1024 * 1024 * 2048, bytes_accessed=24 * 2**20, transcendentals=0),
    )(jnp.stack(a_places + b_places).astype(jnp.int32), *arrays, *b_pieces, *([acc] * has_acc))


def local(t2_slab, lambda_block):
    y, row, col = (lax.axis_index(a) for a in AXES)
    xh, c, xl, z = row // 2, row % 2, col // 4, col % 4
    sgn = 2 * c - 1

    def block(at):
        return lax.dynamic_slice(t2_slab, (lax.rem(at + 8, 4) * 1024, 0), (1024, 128))[None]

    a0 = block(y)
    a1 = send(block(y - sgn), Y_RING)
    a3 = send(block(y + sgn), Y_BACK)
    a2 = send(block(y + 2), Y_FAR)
    o0 = send(a0, XL)
    rest = jnp.concatenate([a1, a2, a3])
    o_rest = send(rest, XL)
    groups = [a0, jnp.concatenate([o0, rest]), o_rest]
    where = {(0, 0): (0, 0), (0, 1): (1, 0)}
    for t in (1, 2, 3):
        where[t, 0], where[t, 1] = (1, t), (2, t - 1)
    steps = [groups]
    for _ in range(3):
        steps.append([send(g, Z_RING) for g in steps[-1]])

    b = [lambda_block]
    for _ in range(3):
        b.append(send(b[-1], Y_RING))
    p = [send(b[0], XH)]
    for _ in range(2):
        p.append(send(p[-1], Y_RING))
    p.append(send(b[3], XH))

    acc = None
    for s in (0, 2, 1, 3):
        pieces, a_places = [], []
        for t in sorted({s, -s % 4}):
            for other in (0, 1):
                h = jnp.abs(xl - other)
                for r in range(4):
                    group, part = where[t, other]
                    pieces.append((steps[r][group], part))
                    zz = lax.rem(z + r * sgn + 8, 4)
                    half = jnp.abs(zz // 2 - c)
                    at = h * 4 + half * 2 + zz % 2
                    if s % 2:
                        at = at + 8 * (half if t == s else 1 - half)
                    a_places.append(at)
        swapped = [send(v, CORE) for v in (b[s], p[s])]
        b_pieces = [b[s], p[s], *swapped]
        b_places = [xh * 2, (1 - xh) * 2, xh * 2 + 1, (1 - xh) * 2 + 1]
        acc = multiply(acc, pieces, a_places, b_pieces, b_places, jnp.bfloat16 if s == 3 else jnp.float32)
    return acc


def solution(mesh):
    placed = (P("row", ("layer", "col")), P(("layer", "row"), "col"))
    return jax.shard_map(
        local, mesh=mesh, in_specs=placed, out_specs=P(("row", "layer"), "col"), check_vma=False
    )
```

time: 329 us -> 173 us (0.53)
  waiting for transfers between devices: 293 us -> 45 us
  starting transfers between devices: 0.08 us -> 56.3 us
  Pallas kernels: 0 us -> 44.9 us
  local copies, waits for them, and re-layouts: 0 us -> 25.6 us
  matrix products: 23.5 us -> 0 us
  between operations: 13.1 us -> 0.35 us
    reduce_scatter x1 -> x0, waiting for transfers between devices: 152 us -> none  [local(): lax.psum_scatter(jnp.dot(amplitude, lambda_layer, preferred_element_type=...]
    all_gather x2 -> x0, waiting for transfers between devices: 139 us -> none  [the longest x1 96 us: local(): amplitude = lax.all_gather(t2_slab, 'col', axis=1, tiled=True)]
    ppermute x0 -> x29, starting transfers between devices: none -> 56.3 us  [send(): return lax.ppermute(x, AXES, perm)]
    ppermute x0 -> x29, waiting for transfers between devices: none -> 45 us  [send(): return lax.ppermute(x, AXES, perm)]
    pallas_call x0 -> x4, Pallas kernels: none -> 44.9 us  [multiply(): pl.pallas_call(kernel, grid_spec=pltpu.PrefetchScalarGridSpec(num_scalar_...]
    unnamed x0 -> x53, local copies, waits for them, and re-layouts: none -> 24 us
    dot_general x1 -> x0, matrix products: 23.5 us -> none  [local(): jnp.dot(amplitude, lambda_layer, preferred_element_type=jnp.float32)]
  transfers between devices with their start and end apart: 3 -> 29, of which waited for: 3 -> 10; matrix products, arithmetic and copies ran while one was open for 0% -> 1% of each run, Pallas kernels for 0% -> 19%
where the time goes in v1:
time: 173 us; the launch traced here: 172 us
  starting transfers between devices  56.3 us (33%)
  waiting for transfers between devices  45 us (26%)
  Pallas kernels  44.9 us (26%)
  local copies, waits for them, and re-layouts  25.6 us (15%)
    ppermute x29, starting transfers between devices, send(): return lax.ppermute(x, AXES, perm)  56.3 us
    ppermute x29, waiting for transfers between devices, send(): return lax.ppermute(x, AXES, perm)  45 us
    pallas_call x4, Pallas kernels, multiply(): pl.pallas_call(kernel, grid_spec=pltpu.PrefetchScalarGridSpec(num_scalar_...  44.9 us
    unnamed x53, local copies, waits for them, and re-layouts  24 us
  transfers between devices with their start and end apart: 29, of which 10 were waited for; matrix products, arithmetic and copies ran while one was open for 1% of the time, Pallas kernels for 19%

profile of v1, /device:TPU:1, one launch (start us, length us, event | category | flops | bytes accessed | tf_op | source)
XLA Modules:
  0.0 172.3 jit_solution(3216114555631546093)
XLA Ops:
  0.0 3.6 %collective-permute-start.11 = (bf16[256,2048]{1,0:T(8,128)(2,1)}, bf16[256,2048]{1,0:T(8,128)(2,1)}, u32[]{:S(2)}, u32[]{:S(2)}) collective-permute-start(bf16[256,2048]{1,0:T(8,128)(2,1)} %refs_8_.1), channel_id=1, source_target_pairs={{0,32},{1,33},{2,34},{3,35},{4,36},{5,37},{6,38},{7,39},{8,104},{9... | collective-permute-start | bytes 3145736 | tf_op jit(solution)/shard_map/ppermute | solution.py:39
  3.6 1.3 dynamic-slice_bitcast_fusion
  4.8 1.3 collective-permute-start
  6.1 0.5 collective-permute-start.1
  6.6 3.8 %collective-permute-start.24 = (bf16[1,1024,128]{2,1,0:T(8,128)(2,1)S(1)}, bf16[1,1024,128]{2,1,0:T(8,128)(2,1)S(1)}, u32[]{:S(2)}, u32[]{:S(2)}) collective-permute-start(bf16[1,1024,128]{2,1,0:T(8,128)(2,1)S(1)} %get-tuple-element.7.refs_0_), channel_id=1, source_target_pairs={{0,1},{1,2},{2,3},{3,0},{4,5},{5,6},{6,7},{7,4},{8,11},{9,8},{10,9... | collective-permute-start | bytes 786440 | tf_op jit(solution)/shard_map/ppermute | solution.py:39
  10.3 0.1 collective-permute-start.2
  10.4 2.9 %collective-permute-done = bf16[1,1024,128]{2,1,0:T(8,128)(2,1)S(1)} collective-permute-done((bf16[1,1024,128]{2,1,0:T(8,128)(2,1)S(1)}, bf16[1,1024,128]{2,1,0:T(8,128)(2,1)S(1)}, u32[]{:S(2)}, u32[]{:S(2)}) %collective-permute-start) | collective-permute-done | bytes 262176 | tf_op jit(solution)/shard_map/ppermute | solution.py:39
  13.3 2.7 %collective-permute-start.17 = (bf16[256,2048]{1,0:T(8,128)(2,1)}, bf16[256,2048]{1,0:T(8,128)(2,1)S(1)}, u32[]{:S(2)}, u32[]{:S(2)}) collective-permute-start(bf16[256,2048]{1,0:T(8,128)(2,1)} %refs_8_.1), channel_id=1, source_target_pairs={{0,16},{1,17},{2,18},{3,19},{4,20},{5,21},{6,22},{7,23},{8,24},{9,... | collective-permute-start | bytes 3145736 | tf_op jit(solution)/shard_map/ppermute | solution.py:39
  16.1 7.9 %collective-permute-done.1 = bf16[1,1024,128]{2,1,0:T(8,128)(2,1)S(1)} collective-permute-done((bf16[1,1024,128]{2,1,0:T(8,128)(2,1)S(1)}, bf16[1,1024,128]{2,1,0:T(8,128)(2,1)S(1)}, u32[]{:S(2)}, u32[]{:S(2)}) %collective-permute-start.1) | collective-permute-done | bytes 262176 | tf_op jit(solution)/shard_map/ppermute | solution.py:39
  24.0 3.8 %collective-permute-start.25 = (bf16[1,1024,128]{2,1,0:T(8,128)(2,1)S(1)}, bf16[1,1024,128]{2,1,0:T(8,128)(2,1)S(1)}, u32[]{:S(2)}, u32[]{:S(2)}) collective-permute-start(bf16[1,1024,128]{2,1,0:T(8,128)(2,1)S(1)} %collective-permute-done.24.refs_1_), channel_id=1, source_target_pairs={{0,1},{1,2},{2,3},{3,0},{4,5},{5,6},{6,7},{7,4},{8,11},{9,8},{10,9... | collective-permute-start | bytes 786440 | tf_op jit(solution)/shard_map/ppermute | solution.py:39
  27.9 0.1 collective-permute-start.27
  28.0 3.1 %collective-permute-done.25.refs_2_ = bf16[1,1024,128]{2,1,0:T(8,128)(2,1)S(1)} collective-permute-done((bf16[1,1024,128]{2,1,0:T(8,128)(2,1)S(1)}, bf16[1,1024,128]{2,1,0:T(8,128)(2,1)S(1)}, u32[]{:S(2)}, u32[]{:S(2)}) %collective-permute-start.25) | collective-permute-done | bytes 262176 | tf_op jit(solution)/shard_map/ppermute | solution.py:39
  31.1 3.4 %collective-permute-start.26 = (bf16[1,1024,128]{2,1,0:T(8,128)(2,1)S(1)}, bf16[1,1024,128]{2,1,0:T(8,128)(2,1)S(1)}, u32[]{:S(2)}, u32[]{:S(2)}) collective-permute-start(bf16[1,1024,128]{2,1,0:T(8,128)(2,1)S(1)} %collective-permute-done.25.refs_2_), channel_id=1, source_target_pairs={{0,1},{1,2},{2,3},{3,0},{4,5},{5,6},{6,7},{7,4},{8,11},{9,8},{10,9... | collective-permute-start | bytes 786440 | tf_op jit(solution)/shard_map/ppermute | solution.py:39
  34.6 0.7 collective-permute-start.4
  35.3 0.1 pad_maximum_fusion
  35.4 2.5 %collective-permute-done.26.refs_3_ = bf16[1,1024,128]{2,1,0:T(8,128)(2,1)S(1)} collective-permute-done((bf16[1,1024,128]{2,1,0:T(8,128)(2,1)S(1)}, bf16[1,1024,128]{2,1,0:T(8,128)(2,1)S(1)}, u32[]{:S(2)}, u32[]{:S(2)}) %collective-permute-start.26) | collective-permute-done | bytes 262176 | tf_op jit(solution)/shard_map/ppermute | solution.py:39
  37.8 0.7 copy-done.23
  38.5 1.1 collective-permute-start.7
  39.6 3.3 %collective-permute-start.12 = (bf16[256,2048]{1,0:T(8,128)(2,1)}, bf16[256,2048]{1,0:T(8,128)(2,1)S(1)}, u32[]{:S(2)}, u32[]{:S(2)}) collective-permute-start(bf16[256,2048]{1,0:T(8,128)(2,1)} %collective-permute-done.11.refs_8_), channel_id=1, source_target_pairs={{0,32},{1,33},{2,34},{3,35},{4,36},{5,37},{6,38},{7,39},{8,104},{9... | collective-permute-start | bytes 3145736 | tf_op jit(solution)/shard_map/ppermute | solution.py:39
  42.9 1.4 collective-permute-start.18
  44.3 10.0 %collective-permute-done.7.refs_4_ = bf16[3,1024,128]{2,1,0:T(8,128)(2,1)S(1)} collective-permute-done((bf16[3,1024,128]{2,1,0:T(8,128)(2,1)S(1)}, bf16[3,1024,128]{2,1,0:T(8,128)(2,1)S(1)}, u32[]{:S(2)}, u32[]{:S(2)}) %collective-permute-start.7) | collective-permute-done | bytes 786464 | tf_op jit(solution)/shard_map/ppermute | solution.py:39
  54.3 6.5 %collective-permute-start.8 = (bf16[3,1024,128]{2,1,0:T(8,128)(2,1)S(1)}, bf16[3,1024,128]{2,1,0:T(8,128)(2,1)S(1)}, u32[]{:S(2)}, u32[]{:S(2)}) collective-permute-start(bf16[3,1024,128]{2,1,0:T(8,128)(2,1)S(1)} %collective-permute-done.7.refs_4_), channel_id=1, source_target_pairs={{0,1},{1,2},{2,3},{3,0},{4,5},{5,6},{6,7},{7,4},{8,11},{9,8},{10,9... | collective-permute-start | bytes 2359304 | tf_op jit(solution)/shard_map/ppermute | solution.py:39
  60.8 0.9 copy-done.4
  61.7 1.0 copy-done.11
  62.7 1.0 copy-done.9
  63.6 1.2 collective-permute-start.5
  64.8 3.1 %collective-permute-start.13 = (bf16[256,2048]{1,0:T(8,128)(2,1)S(1)}, bf16[256,2048]{1,0:T(8,128)(2,1)}, u32[]{:S(2)}, u32[]{:S(2)}) collective-permute-start(bf16[256,2048]{1,0:T(8,128)(2,1)S(1)} %collective-permute-done.12.refs_8_), channel_id=1, source_target_pairs={{0,32},{1,33},{2,34},{3,35},{4,36},{5,37},{6,38},{7,39},{8,104},{9... | collective-permute-start | bytes 3145736 | tf_op jit(solution)/shard_map/ppermute | solution.py:39
  67.9 1.5 collective-permute-start.21
  69.5 0.2 collective-permute-done.8.refs_5_
  69.7 3.5 %collective-permute-start.9 = (bf16[3,1024,128]{2,1,0:T(8,128)(2,1)S(1)}, bf16[3,1024,128]{2,1,0:T(8,128)(2,1)}, u32[]{:S(2)}, u32[]{:S(2)}) collective-permute-start(bf16[3,1024,128]{2,1,0:T(8,128)(2,1)S(1)} %collective-permute-done.8.refs_5_), channel_id=1, source_target_pairs={{0,1},{1,2},{2,3},{3,0},{4,5},{5,6},{6,7},{7,4},{8,11},{9,8},{10,9... | collective-permute-start | bytes 2359304 | tf_op jit(solution)/shard_map/ppermute | solution.py:39
  73.2 0.9 copy-done.6
  74.1 1.0 copy-done.13
  75.1 1.0 copy-done.15
  76.0 4.9 %collective-permute-done.5.refs_6_.refs_2_ = bf16[4,1024,128]{2,1,0:T(8,128)(2,1)S(1)} collective-permute-done((bf16[4,1024,128]{2,1,0:T(8,128)(2,1)S(1)}, bf16[4,1024,128]{2,1,0:T(8,128)(2,1)S(1)}, u32[]{:S(2)}, u32[]{:S(2)}) %collective-permute-start.5) | collective-permute-done | bytes 1048608 | tf_op jit(solution)/shard_map/ppermute | solution.py:39
  80.9 3.5 %collective-permute-start.6 = (bf16[4,1024,128]{2,1,0:T(8,128)(2,1)S(1)}, bf16[4,1024,128]{2,1,0:T(8,128)(2,1)S(1)}, u32[]{:S(2)}, u32[]{:S(2)}) collective-permute-start(bf16[4,1024,128]{2,1,0:T(8,128)(2,1)S(1)} %collective-permute-done.5.refs_6_.refs_2_), channel_id=1, source_target_pairs={{0,1},{1,2},{2,3},{3,0},{4,5},{5,6},{6,7},{7,4},{8,11},{9,8},{10,9... | collective-permute-start | bytes 3145736 | tf_op jit(solution)/shard_map/ppermute | solution.py:39
  84.4 2.1 %collective-permute-start.14 = (bf16[256,2048]{1,0:T(8,128)(2,1)}, bf16[256,2048]{1,0:T(8,128)(2,1)}, u32[]{:S(2)}, u32[]{:S(2)}) collective-permute-start(bf16[256,2048]{1,0:T(8,128)(2,1)} %collective-permute-done.13.refs_8_), channel_id=1, source_target_pairs={{0,16},{1,17},{2,18},{3,19},{4,20},{5,21},{6,22},{7,23},{8,24},{9,... | collective-permute-start | bytes 3145736 | tf_op jit(solution)/shard_map/ppermute | solution.py:39
  86.5 2.8 %collective-permute-done.9.refs_6_ = bf16[3,1024,128]{2,1,0:T(8,128)(2,1)} collective-permute-done((bf16[3,1024,128]{2,1,0:T(8,128)(2,1)S(1)}, bf16[3,1024,128]{2,1,0:T(8,128)(2,1)}, u32[]{:S(2)}, u32[]{:S(2)}) %collective-permute-start.9) | collective-permute-done | bytes 786464 | tf_op jit(solution)/shard_map/ppermute | solution.py:39
  89.3 3.5 %collective-permute-start.10 = (bf16[3,1024,128]{2,1,0:T(8,128)(2,1)}, bf16[3,1024,128]{2,1,0:T(8,128)(2,1)}, u32[]{:S(2)}, u32[]{:S(2)}) collective-permute-start(bf16[3,1024,128]{2,1,0:T(8,128)(2,1)} %collective-permute-done.9.refs_6_), channel_id=1, source_target_pairs={{0,1},{1,2},{2,3},{3,0},{4,5},{5,6},{6,7},{7,4},{8,11},{9,8},{10,9... | collective-permute-start | bytes 2359304 | tf_op jit(solution)/shard_map/ppermute | solution.py:39
  92.9 0.8 collective-permute-start.23
  93.7 1.0 copy-done.17
  94.7 0.0 collective-permute-start.19
  94.7 5.9 %collective-permute-done.6.refs_7_.refs_3_ = bf16[4,1024,128]{2,1,0:T(8,128)(2,1)S(1)} collective-permute-done((bf16[4,1024,128]{2,1,0:T(8,128)(2,1)S(1)}, bf16[4,1024,128]{2,1,0:T(8,128)(2,1)S(1)}, u32[]{:S(2)}, u32[]{:S(2)}) %collective-permute-start.6) | collective-permute-done | bytes 1048608 | tf_op jit(solution)/shard_map/ppermute | solution.py:39
  100.6 1.0 copy-done.2
  101.6 2.5 %collective-permute-start.20 = (bf16[256,2048]{1,0:T(8,128)(2,1)}, bf16[256,2048]{1,0:T(8,128)(2,1)}, u32[]{:S(2)}, u32[]{:S(2)}) collective-permute-start(bf16[256,2048]{1,0:T(8,128)(2,1)} %collective-permute-done.18.refs_9_), channel_id=1, source_target_pairs={{0,8},{1,9},{2,10},{3,11},{4,12},{5,13},{6,14},{7,15},{8,0},{9,1},... | collective-permute-start | bytes 3145736 | tf_op jit(solution)/shard_map/ppermute | solution.py:39
  104.0 0.1 stack.151.place_ref
  104.1 0.1 stack.150.place_ref
  104.2 0.1 stack.160.place_ref
  104.3 4.8 %collective-permute-done.10.refs_7_ = bf16[3,1024,128]{2,1,0:T(8,128)(2,1)} collective-permute-done((bf16[3,1024,128]{2,1,0:T(8,128)(2,1)}, bf16[3,1024,128]{2,1,0:T(8,128)(2,1)}, u32[]{:S(2)}, u32[]{:S(2)}) %collective-permute-start.10) | collective-permute-done | bytes 786464 | tf_op jit(solution)/shard_map/ppermute | solution.py:39
  109.1 2.5 %collective-permute-start.15 = (bf16[256,2048]{1,0:T(8,128)(2,1)}, bf16[256,2048]{1,0:T(8,128)(2,1)}, u32[]{:S(2)}, u32[]{:S(2)}) collective-permute-start(bf16[256,2048]{1,0:T(8,128)(2,1)} %collective-permute-done.13.refs_8_), channel_id=1, source_target_pairs={{0,8},{1,9},{2,10},{3,11},{4,12},{5,13},{6,14},{7,15},{8,0},{9,1},... | collective-permute-start | bytes 3145736 | tf_op jit(solution)/shard_map/ppermute | solution.py:39
  111.6 0.0 collective-permute-start.16
  111.6 1.2 copy-done.3
  112.8 1.2 copy-done.8
  114.1 1.2 copy-done.10
  115.3 1.2 copy-done.12
  116.5 1.2 copy-done.14
  117.7 0.9 copy-done.20
  118.7 0.9 copy-done.22
  119.6 0.9 copy-done.24
  120.6 8.1 %shard_map.28.refs_12_ = f32[1024,2048]{1,0:T(8,128)S(1)} custom-call(s32[12]{0:T(128)S(1)} %stack.160.place_ref, bf16[1,1024,128]{2,1,0:T(8,128)(2,1)S(1)} %get-tuple-element.7.refs_0_, bf16[1,1024,128]{2,1,0:T(8,128)(2,1)S(1)} %copy-done.20, bf16[1,1024,128]{2,1,0:T(8,128)(2,1)S(1)} %copy-done.22, bf16[1,1024,128]{2,1,0:T(8,128)(2,1)S(1)} %copy-done.24, ...), custom_call_target="tpu_custom_call" | custom-call | flops 4294967296 | bytes 25165824 | tf_op jit(solution)/shard_map/pallas_call | solution.py:81
  128.7 3.3 %copy-done = f32[1024,2048]{1,0:T(8,128)} copy-done((f32[1024,2048]{1,0:T(8,128)}, f32[1024,2048]{1,0:T(8,128)S(1)}, u32[]{:S(2)}) %copy-start) | copy-done | bytes 8388632
  132.0 12.1 %shard_map.29.refs_12_ = f32[1024,2048]{1,0:T(8,128)S(1)} custom-call(s32[12]{0:T(128)S(1)} %stack.160.place_ref, bf16[4,1024,128]{2,1,0:T(8,128)(2,1)S(1)} %constant_dynamic-update-slice_fusion.refs_4_.refs_0_, bf16[4,1024,128]{2,1,0:T(8,128)(2,1)S(1)} %collective-permute-done.4.refs_5_.refs_1_, ...), custom_call_target="tpu_custom_call" | custom-call | flops 4294967296 | bytes 25165824 | tf_op jit(solution)/shard_map/pallas_call | solution.py:81
  144.1 3.3 %copy-done.1 = f32[1024,2048]{1,0:T(8,128)} copy-done((f32[1024,2048]{1,0:T(8,128)}, f32[1024,2048]{1,0:T(8,128)S(1)}, u32[]{:S(2)}) %copy-start.1) | copy-done | bytes 8388632
  147.4 13.2 %shard_map.30.refs_12_ = f32[1024,2048]{1,0:T(8,128)S(1)} custom-call(s32[20]{0:T(128)S(1)} %stack.151.place_ref, bf16[4,1024,128]{2,1,0:T(8,128)(2,1)S(1)} %constant_dynamic-update-slice_fusion.refs_4_.refs_0_, bf16[4,1024,128]{2,1,0:T(8,128)(2,1)S(1)} %collective-permute-done.4.refs_5_.refs_1_, ...), custom_call_target="tpu_custom_call" | custom-call | flops 4294967296 | bytes 25165824 | tf_op jit(solution)/shard_map/pallas_call | solution.py:81
  160.7 11.5 %shard_map.31 = bf16[1024,2048]{1,0:T(8,128)(2,1)} custom-call(s32[20]{0:T(128)S(1)} %stack.150.place_ref, bf16[4,1024,128]{2,1,0:T(8,128)(2,1)S(1)} %constant_dynamic-update-slice_fusion.refs_4_.refs_0_, bf16[4,1024,128]{2,1,0:T(8,128)(2,1)S(1)} %collective-permute-done.4.refs_5_.refs_1_, bf16[4,1024,128]{2,1,0:T(8,128)(2,1)S(1)} %collective-permute-done.5.refs_6_.refs_2_, ...), custom_call_target="tpu_custom_call" | custom-call | flops 4294967296 | bytes 25165824 | tf_op jit(solution)/shard_map/pallas_call | solution.py:81
  (57 shorter events, 0.2 us)
Async XLA Ops:
  0.0 39.6 %collective-permute-start.11 = (bf16[256,2048]{1,0:T(8,128)(2,1)}, bf16[256,2048]{1,0:T(8,128)(2,1)}, u32[]{:S(2)}, u32[]{:S(2)}) collective-permute-start(bf16[256,2048]{1,0:T(8,128)(2,1)} %refs_8_.1), channel_id=1, source_target_pairs={{0,32},{1,33},{2,34},{3,35},{4,36},{5,37},{6,38},{7,39},{8,104},{9... | collective-permute-start | bytes 3145736 | tf_op jit(solution)/shard_map/ppermute | solution.py:39
  4.8 8.5 %collective-permute-start = (bf16[1,1024,128]{2,1,0:T(8,128)(2,1)S(1)}, bf16[1,1024,128]{2,1,0:T(8,128)(2,1)S(1)}, u32[]{:S(2)}, u32[]{:S(2)}) collective-permute-start(bf16[1,1024,128]{2,1,0:T(8,128)(2,1)S(1)} %get-tuple-element.7.refs_0_), channel_id=1, source_target_pairs={{0,4},{1,5},{2,6},{3,7},{4,0},{5,1},{6,2},{7,3},{8,12},{9,13},{10,... | collective-permute-start | bytes 786440 | tf_op jit(solution)/shard_map/ppermute | solution.py:39
  6.1 17.8 %collective-permute-start.1 = (bf16[1,1024,128]{2,1,0:T(8,128)(2,1)S(1)}, bf16[1,1024,128]{2,1,0:T(8,128)(2,1)S(1)}, u32[]{:S(2)}, u32[]{:S(2)}) collective-permute-start(bf16[1,1024,128]{2,1,0:T(8,128)(2,1)S(1)} %get-tuple-element.6), channel_id=1, source_target_pairs={{0,32},{1,33},{2,34},{3,35},{4,36},{5,37},{6,38},{7,39},{8,104},{9... | collective-permute-start | bytes 786440 | tf_op jit(solution)/shard_map/ppermute | solution.py:39
  6.6 17.4 %collective-permute-start.24 = (bf16[1,1024,128]{2,1,0:T(8,128)(2,1)S(1)}, bf16[1,1024,128]{2,1,0:T(8,128)(2,1)S(1)}, u32[]{:S(2)}, u32[]{:S(2)}) collective-permute-start(bf16[1,1024,128]{2,1,0:T(8,128)(2,1)S(1)} %get-tuple-element.7.refs_0_), channel_id=1, source_target_pairs={{0,1},{1,2},{2,3},{3,0},{4,5},{5,6},{6,7},{7,4},{8,11},{9,8},{10,9... | collective-permute-start | bytes 786440 | tf_op jit(solution)/shard_map/ppermute | solution.py:39
  10.3 17.5 %collective-permute-start.2 = (bf16[1,1024,128]{2,1,0:T(8,128)(2,1)S(1)}, bf16[1,1024,128]{2,1,0:T(8,128)(2,1)S(1)}, u32[]{:S(2)}, u32[]{:S(2)}) collective-permute-start(bf16[1,1024,128]{2,1,0:T(8,128)(2,1)S(1)} %get-tuple-element.8), channel_id=1, source_target_pairs={{0,64},{1,65},{2,66},{3,67},{4,68},{5,69},{6,70},{7,71},{8,72},{9,... | collective-permute-start | bytes 786440 | tf_op jit(solution)/shard_map/ppermute | solution.py:39
  13.3 29.5 %collective-permute-start.17 = (bf16[256,2048]{1,0:T(8,128)(2,1)}, bf16[256,2048]{1,0:T(8,128)(2,1)S(1)}, u32[]{:S(2)}, u32[]{:S(2)}) collective-permute-start(bf16[256,2048]{1,0:T(8,128)(2,1)} %refs_8_.1), channel_id=1, source_target_pairs={{0,16},{1,17},{2,18},{3,19},{4,20},{5,21},{6,22},{7,23},{8,24},{9,... | collective-permute-start | bytes 3145736 | tf_op jit(solution)/shard_map/ppermute | solution.py:39
  23.9 10.6 %collective-permute-start.3 = (bf16[1,1024,128]{2,1,0:T(8,128)(2,1)S(1)}, bf16[1,1024,128]{2,1,0:T(8,128)(2,1)S(1)}, u32[]{:S(2)}, u32[]{:S(2)}) collective-permute-start(bf16[1,1024,128]{2,1,0:T(8,128)(2,1)S(1)} %get-tuple-element.5), channel_id=1, source_target_pairs={{0,96},{1,97},{2,98},{3,99},{4,100},{5,101},{6,102},{7,103},{8,40}... | collective-permute-start | bytes 786440 | tf_op jit(solution)/shard_map/ppermute | solution.py:39
  24.0 10.6 %copy-start.19 = (bf16[1,1024,128]{2,1,0:T(8,128)(2,1)}, bf16[1,1024,128]{2,1,0:T(8,128)(2,1)S(1)}, u32[]{:S(2)}) copy-start(bf16[1,1024,128]{2,1,0:T(8,128)(2,1)S(1)} %collective-permute-done.24.refs_1_) | copy-start | bytes 786436
  24.0 7.1 %collective-permute-start.25 = (bf16[1,1024,128]{2,1,0:T(8,128)(2,1)S(1)}, bf16[1,1024,128]{2,1,0:T(8,128)(2,1)S(1)}, u32[]{:S(2)}, u32[]{:S(2)}) collective-permute-start(bf16[1,1024,128]{2,1,0:T(8,128)(2,1)S(1)} %collective-permute-done.24.refs_1_), channel_id=1, source_target_pairs={{0,1},{1,2},{2,3},{3,0},{4,5},{5,6},{6,7},{7,4},{8,11},{9,8},{10,9... | collective-permute-start | bytes 786440 | tf_op jit(solution)/shard_map/ppermute | solution.py:39
  27.9 33.8 %collective-permute-start.27 = (bf16[256,2048]{1,0:T(8,128)(2,1)}, bf16[256,2048]{1,0:T(8,128)(2,1)S(1)}, u32[]{:S(2)}, u32[]{:S(2)}) collective-permute-start(bf16[256,2048]{1,0:T(8,128)(2,1)} %refs_8_.1), channel_id=1, source_target_pairs={{0,8},{1,9},{2,10},{3,11},{4,12},{5,13},{6,14},{7,15},{8,0},{9,1},... | collective-permute-start | bytes 3145736 | tf_op jit(solution)/shard_map/ppermute | solution.py:39
  31.1 69.5 %copy-start.21 = (bf16[1,1024,128]{2,1,0:T(8,128)(2,1)}, bf16[1,1024,128]{2,1,0:T(8,128)(2,1)S(1)}, u32[]{:S(2)}) copy-start(bf16[1,1024,128]{2,1,0:T(8,128)(2,1)S(1)} %collective-permute-done.25.refs_2_) | copy-start | bytes 786436
  31.1 6.7 %collective-permute-start.26 = (bf16[1,1024,128]{2,1,0:T(8,128)(2,1)S(1)}, bf16[1,1024,128]{2,1,0:T(8,128)(2,1)S(1)}, u32[]{:S(2)}, u32[]{:S(2)}) collective-permute-start(bf16[1,1024,128]{2,1,0:T(8,128)(2,1)S(1)} %collective-permute-done.25.refs_2_), channel_id=1, source_target_pairs={{0,1},{1,2},{2,3},{3,0},{4,5},{5,6},{6,7},{7,4},{8,11},{9,8},{10,9... | collective-permute-start | bytes 786440 | tf_op jit(solution)/shard_map/ppermute | solution.py:39
  34.6 29.1 %collective-permute-start.4 = (bf16[4,1024,128]{2,1,0:T(8,128)(2,1)S(1)}, bf16[4,1024,128]{2,1,0:T(8,128)(2,1)S(1)}, u32[]{:S(2)}, u32[]{:S(2)}) collective-permute-start(bf16[4,1024,128]{2,1,0:T(8,128)(2,1)S(1)} %constant_dynamic-update-slice_fusion.refs_4_.refs_0_), channel_id=1, source_target_pairs={{0,1},{1,2},{2,3},{3,0},{4,5},{5,6},{6,7},{7,4},{8,11},{9,8},{10,9... | collective-permute-start | bytes 3145736 | tf_op jit(solution)/shard_map/ppermute | solution.py:39
  37.8 0.7 copy-start.23
  38.5 15.7 %collective-permute-start.7 = (bf16[3,1024,128]{2,1,0:T(8,128)(2,1)S(1)}, bf16[3,1024,128]{2,1,0:T(8,128)(2,1)S(1)}, u32[]{:S(2)}, u32[]{:S(2)}) collective-permute-start(bf16[3,1024,128]{2,1,0:T(8,128)(2,1)S(1)} %pad_maximum_fusion), channel_id=1, source_target_pairs={{0,4},{1,5},{2,6},{3,7},{4,0},{5,1},{6,2},{7,3},{8,12},{9,13},{10,... | collective-permute-start | bytes 2359304 | tf_op jit(solution)/shard_map/ppermute | solution.py:39
  39.6 25.2 %collective-permute-start.12 = (bf16[256,2048]{1,0:T(8,128)(2,1)}, bf16[256,2048]{1,0:T(8,128)(2,1)S(1)}, u32[]{:S(2)}, u32[]{:S(2)}) collective-permute-start(bf16[256,2048]{1,0:T(8,128)(2,1)} %collective-permute-done.11.refs_8_), channel_id=1, source_target_pairs={{0,32},{1,33},{2,34},{3,35},{4,36},{5,37},{6,38},{7,39},{8,104},{9... | collective-permute-start | bytes 3145736 | tf_op jit(solution)/shard_map/ppermute | solution.py:39
  42.9 25.1 %collective-permute-start.18 = (bf16[256,2048]{1,0:T(8,128)(2,1)S(1)}, bf16[256,2048]{1,0:T(8,128)(2,1)}, u32[]{:S(2)}, u32[]{:S(2)}) collective-permute-start(bf16[256,2048]{1,0:T(8,128)(2,1)S(1)} %collective-permute-done.17.refs_9_), channel_id=1, source_target_pairs={{0,32},{1,33},{2,34},{3,35},{4,36},{5,37},{6,38},{7,39},{8,104},{9... | collective-permute-start | bytes 3145736 | tf_op jit(solution)/shard_map/ppermute | solution.py:39
  54.3 15.4 %collective-permute-start.8 = (bf16[3,1024,128]{2,1,0:T(8,128)(2,1)S(1)}, bf16[3,1024,128]{2,1,0:T(8,128)(2,1)S(1)}, u32[]{:S(2)}, u32[]{:S(2)}) collective-permute-start(bf16[3,1024,128]{2,1,0:T(8,128)(2,1)S(1)} %collective-permute-done.7.refs_4_), channel_id=1, source_target_pairs={{0,1},{1,2},{2,3},{3,0},{4,5},{5,6},{6,7},{7,4},{8,11},{9,8},{10,9... | collective-permute-start | bytes 2359304 | tf_op jit(solution)/shard_map/ppermute | solution.py:39
  60.8 0.9 copy-start.4
  61.7 1.0 copy-start.11
  62.7 11.4 %collective-permute-start.28 = (bf16[256,2048]{1,0:T(8,128)(2,1)S(1)}, bf16[256,2048]{1,0:T(8,128)(2,1)S(1)}, u32[]{:S(2)}, u32[]{:S(2)}) collective-permute-start(bf16[256,2048]{1,0:T(8,128)(2,1)S(1)} %collective-permute-done.17.refs_9_), channel_id=1, source_target_pairs={{0,8},{1,9},{2,10},{3,11},{4,12},{5,13},{6,14},{7,15},{8,0},{9,1},... | collective-permute-start | bytes 3145736 | tf_op jit(solution)/shard_map/ppermute | solution.py:39
  62.7 1.0 copy-start.9
  63.6 17.3 %collective-permute-start.5 = (bf16[4,1024,128]{2,1,0:T(8,128)(2,1)S(1)}, bf16[4,1024,128]{2,1,0:T(8,128)(2,1)S(1)}, u32[]{:S(2)}, u32[]{:S(2)}) collective-permute-start(bf16[4,1024,128]{2,1,0:T(8,128)(2,1)S(1)} %collective-permute-done.4.refs_5_.refs_1_), channel_id=1, source_target_pairs={{0,1},{1,2},{2,3},{3,0},{4,5},{5,6},{6,7},{7,4},{8,11},{9,8},{10,9... | collective-permute-start | bytes 3145736 | tf_op jit(solution)/shard_map/ppermute | solution.py:39
  64.8 19.6 %collective-permute-start.13 = (bf16[256,2048]{1,0:T(8,128)(2,1)S(1)}, bf16[256,2048]{1,0:T(8,128)(2,1)}, u32[]{:S(2)}, u32[]{:S(2)}) collective-permute-start(bf16[256,2048]{1,0:T(8,128)(2,1)S(1)} %collective-permute-done.12.refs_8_), channel_id=1, source_target_pairs={{0,32},{1,33},{2,34},{3,35},{4,36},{5,37},{6,38},{7,39},{8,104},{9... | collective-permute-start | bytes 3145736 | tf_op jit(solution)/shard_map/ppermute | solution.py:39
  67.9 24.9 %collective-permute-start.21 = (bf16[256,2048]{1,0:T(8,128)(2,1)}, bf16[256,2048]{1,0:T(8,128)(2,1)}, u32[]{:S(2)}, u32[]{:S(2)}) collective-permute-start(bf16[256,2048]{1,0:T(8,128)(2,1)} %collective-permute-done.18.refs_9_), channel_id=1, source_target_pairs={{0,32},{1,33},{2,34},{3,35},{4,36},{5,37},{6,38},{7,39},{8,104},{9... | collective-permute-start | bytes 3145736 | tf_op jit(solution)/shard_map/ppermute | solution.py:39
  69.7 19.7 %collective-permute-start.9 = (bf16[3,1024,128]{2,1,0:T(8,128)(2,1)S(1)}, bf16[3,1024,128]{2,1,0:T(8,128)(2,1)}, u32[]{:S(2)}, u32[]{:S(2)}) collective-permute-start(bf16[3,1024,128]{2,1,0:T(8,128)(2,1)S(1)} %collective-permute-done.8.refs_5_), channel_id=1, source_target_pairs={{0,1},{1,2},{2,3},{3,0},{4,5},{5,6},{6,7},{7,4},{8,11},{9,8},{10,9... | collective-permute-start | bytes 2359304 | tf_op jit(solution)/shard_map/ppermute | solution.py:39
  73.2 0.9 copy-start.6
  74.1 1.0 copy-start.13
  75.1 18.6 %collective-permute-start.22 = (bf16[256,2048]{1,0:T(8,128)(2,1)S(1)}, bf16[256,2048]{1,0:T(8,128)(2,1)S(1)}, u32[]{:S(2)}, u32[]{:S(2)}) collective-permute-start(bf16[256,2048]{1,0:T(8,128)(2,1)S(1)} %collective-permute-done.12.refs_8_), channel_id=1, source_target_pairs={{0,8},{1,9},{2,10},{3,11},{4,12},{5,13},{6,14},{7,15},{8,0},{9,1},... | collective-permute-start | bytes 3145736 | tf_op jit(solution)/shard_map/ppermute | solution.py:39
  75.1 1.0 copy-start.15
  80.9 19.7 %collective-permute-start.6 = (bf16[4,1024,128]{2,1,0:T(8,128)(2,1)S(1)}, bf16[4,1024,128]{2,1,0:T(8,128)(2,1)S(1)}, u32[]{:S(2)}, u32[]{:S(2)}) collective-permute-start(bf16[4,1024,128]{2,1,0:T(8,128)(2,1)S(1)} %collective-permute-done.5.refs_6_.refs_2_), channel_id=1, source_target_pairs={{0,1},{1,2},{2,3},{3,0},{4,5},{5,6},{6,7},{7,4},{8,11},{9,8},{10,9... | collective-permute-start | bytes 3145736 | tf_op jit(solution)/shard_map/ppermute | solution.py:39
  84.4 27.2 %collective-permute-start.14 = (bf16[256,2048]{1,0:T(8,128)(2,1)}, bf16[256,2048]{1,0:T(8,128)(2,1)}, u32[]{:S(2)}, u32[]{:S(2)}) collective-permute-start(bf16[256,2048]{1,0:T(8,128)(2,1)} %collective-permute-done.13.refs_8_), channel_id=1, source_target_pairs={{0,16},{1,17},{2,18},{3,19},{4,20},{5,21},{6,22},{7,23},{8,24},{9,... | collective-permute-start | bytes 3145736 | tf_op jit(solution)/shard_map/ppermute | solution.py:39
  89.3 19.8 %collective-permute-start.10 = (bf16[3,1024,128]{2,1,0:T(8,128)(2,1)}, bf16[3,1024,128]{2,1,0:T(8,128)(2,1)}, u32[]{:S(2)}, u32[]{:S(2)}) collective-permute-start(bf16[3,1024,128]{2,1,0:T(8,128)(2,1)} %collective-permute-done.9.refs_6_), channel_id=1, source_target_pairs={{0,1},{1,2},{2,3},{3,0},{4,5},{5,6},{6,7},{7,4},{8,11},{9,8},{10,9... | collective-permute-start | bytes 2359304 | tf_op jit(solution)/shard_map/ppermute | solution.py:39
  92.9 39.1 %collective-permute-start.23 = (bf16[256,2048]{1,0:T(8,128)(2,1)}, bf16[256,2048]{1,0:T(8,128)(2,1)}, u32[]{:S(2)}, u32[]{:S(2)}) collective-permute-start(bf16[256,2048]{1,0:T(8,128)(2,1)} %collective-permute-done.21.refs_9_), channel_id=1, source_target_pairs={{0,8},{1,9},{2,10},{3,11},{4,12},{5,13},{6,14},{7,15},{8,0},{9,1},... | collective-permute-start | bytes 3145736 | tf_op jit(solution)/shard_map/ppermute | solution.py:39
  93.7 1.0 copy-start.17
  94.7 52.8 %collective-permute-start.19 = (bf16[256,2048]{1,0:T(8,128)(2,1)}, bf16[256,2048]{1,0:T(8,128)(2,1)}, u32[]{:S(2)}, u32[]{:S(2)}) collective-permute-start(bf16[256,2048]{1,0:T(8,128)(2,1)} %collective-permute-done.11.refs_8_), channel_id=1, source_target_pairs={{0,8},{1,9},{2,10},{3,11},{4,12},{5,13},{6,14},{7,15},{8,0},{9,1},... | collective-permute-start | bytes 3145736 | tf_op jit(solution)/shard_map/ppermute | solution.py:39
  100.6 1.0 copy-start.2
  101.6 45.9 %collective-permute-start.20 = (bf16[256,2048]{1,0:T(8,128)(2,1)}, bf16[256,2048]{1,0:T(8,128)(2,1)}, u32[]{:S(2)}, u32[]{:S(2)}) collective-permute-start(bf16[256,2048]{1,0:T(8,128)(2,1)} %collective-permute-done.18.refs_9_), channel_id=1, source_target_pairs={{0,8},{1,9},{2,10},{3,11},{4,12},{5,13},{6,14},{7,15},{8,0},{9,1},... | collective-permute-start | bytes 3145736 | tf_op jit(solution)/shard_map/ppermute | solution.py:39
  109.1 51.6 %collective-permute-start.15 = (bf16[256,2048]{1,0:T(8,128)(2,1)}, bf16[256,2048]{1,0:T(8,128)(2,1)}, u32[]{:S(2)}, u32[]{:S(2)}) collective-permute-start(bf16[256,2048]{1,0:T(8,128)(2,1)} %collective-permute-done.13.refs_8_), channel_id=1, source_target_pairs={{0,8},{1,9},{2,10},{3,11},{4,12},{5,13},{6,14},{7,15},{8,0},{9,1},... | collective-permute-start | bytes 3145736 | tf_op jit(solution)/shard_map/ppermute | solution.py:39
  111.6 49.1 %collective-permute-start.16 = (bf16[256,2048]{1,0:T(8,128)(2,1)}, bf16[256,2048]{1,0:T(8,128)(2,1)}, u32[]{:S(2)}, u32[]{:S(2)}) collective-permute-start(bf16[256,2048]{1,0:T(8,128)(2,1)} %collective-permute-done.14.refs_9_), channel_id=1, source_target_pairs={{0,8},{1,9},{2,10},{3,11},{4,12},{5,13},{6,14},{7,15},{8,0},{9,1},... | collective-permute-start | bytes 3145736 | tf_op jit(solution)/shard_map/ppermute | solution.py:39
  111.6 1.2 copy-start.3
  112.8 1.2 copy-start.8
  114.0 1.2 copy-start.10
  115.3 1.2 copy-start.12
  116.5 1.2 copy-start.14
  117.7 0.9 copy-start.20
  118.7 0.9 copy-start.22
  119.6 0.9 copy-start.24
  120.6 11.4 %copy-start.5 = (bf16[3,1024,128]{2,1,0:T(8,128)(2,1)S(1)}, bf16[3,1024,128]{2,1,0:T(8,128)(2,1)}, u32[]{:S(2)}) copy-start(bf16[3,1024,128]{2,1,0:T(8,128)(2,1)} %copy-done.4) | copy-start | bytes 2359300
  120.6 11.4 %copy-start.7 = (bf16[3,1024,128]{2,1,0:T(8,128)(2,1)S(1)}, bf16[3,1024,128]{2,1,0:T(8,128)(2,1)}, u32[]{:S(2)}) copy-start(bf16[3,1024,128]{2,1,0:T(8,128)(2,1)} %copy-done.6) | copy-start | bytes 2359300
  120.6 11.4 %copy-start.16 = (bf16[256,2048]{1,0:T(8,128)(2,1)S(1)}, bf16[256,2048]{1,0:T(8,128)(2,1)}, u32[]{:S(2)}) copy-start(bf16[256,2048]{1,0:T(8,128)(2,1)} %copy-done.15) | copy-start | bytes 3145732
  120.6 11.4 %copy-start.18 = (bf16[256,2048]{1,0:T(8,128)(2,1)S(1)}, bf16[256,2048]{1,0:T(8,128)(2,1)}, u32[]{:S(2)}) copy-start(bf16[256,2048]{1,0:T(8,128)(2,1)} %copy-done.17) | copy-start | bytes 3145732
  128.7 3.3 %copy-start = (f32[1024,2048]{1,0:T(8,128)}, f32[1024,2048]{1,0:T(8,128)S(1)}, u32[]{:S(2)}) copy-start(f32[1024,2048]{1,0:T(8,128)S(1)} %shard_map.28.refs_12_) | copy-start | bytes 25165828
  144.1 3.3 %copy-start.1 = (f32[1024,2048]{1,0:T(8,128)}, f32[1024,2048]{1,0:T(8,128)S(1)}, u32[]{:S(2)}) copy-start(f32[1024,2048]{1,0:T(8,128)S(1)} %shard_map.29.refs_12_) | copy-start | bytes 25165828

commit v2 on v0

v2 whole, which is shorter than its diff:
```python
import functools

import jax
import jax.numpy as jnp
from jax import lax
from jax.experimental import pallas as pl
from jax.experimental.pallas import tpu as pltpu
from jax.sharding import PartitionSpec as P

AXES = ("layer", "row", "col")
SPAN = 512


def flat(y, xh, c, xl, z):
    return (y % 4 * 4 + xh % 2 * 2 + c % 2) * 8 + xl % 2 * 4 + z % 4


def pairs(move):
    return [
        (flat(y, xh, c, xl, z), flat(*move(y, xh, c, xl, z)))
        for y in range(4) for xh in range(2) for c in range(2) for xl in range(2) for z in range(4)
    ]


def way(c):
    return 1 if c == 0 else -1


Y_RING = pairs(lambda y, xh, c, xl, z: (y + way(c), xh, c, xl, z))
Y_BACK = pairs(lambda y, xh, c, xl, z: (y - way(c), xh, c, xl, z))
Y_FAR = pairs(lambda y, xh, c, xl, z: (y + 2, xh, c, xl, z))
Z_RING = pairs(lambda y, xh, c, xl, z: (y, xh, c, xl, z + way(c)))
Z_BACK = pairs(lambda y, xh, c, xl, z: (y, xh, c, xl, z - way(c)))
XH = pairs(lambda y, xh, c, xl, z: (y, xh + 1, c, xl, z))
XL = pairs(lambda y, xh, c, xl, z: (y, xh, c, xl + 1, z))
CORE = pairs(lambda y, xh, c, xl, z: (y, xh, c + 1, xl, z))

STEPS = (
    ("A1", ("k1",), Y_RING, ()),
    ("A3", ("k3",), Y_BACK, ()),
    ("A2", ("k2",), Y_FAR, ()),
    ("O0", ("k0",), XL, ()),
    ("P0", ("b0",), XH, ()),
    ("X123", ("A1", "A3", "A2"), XL, ()),
    ("B3", ("b0",), Y_BACK, ()),
    ("B1", ("b0",), Y_RING, ()),
    ("B2", ("B1",), Y_RING, ()),
    ("n0", ("k0", "O0", "A1", "A3"), Z_RING, ()),
    ("c0", ("k0", "O0", "A1", "A3"), Z_BACK, ()),
    ("f0", ("n0",), Z_RING, ()),
    ("c1", ("A2", "X123"), Z_BACK, ()),
    ("Cb0", ("b0",), CORE, ()),
    ("CP0", ("P0",), CORE, ()),
    ("CB3", ("B3",), CORE, ()),
    ("M0", (0,), 0.01, ()),
    ("Q1", ("P0",), Y_RING, ("c0",)),
    ("Q2", ("Q1",), Y_RING, ("f0", "X123", "A2")),
    ("P3", ("B3",), XH, ("n0",)),
    ("n1", ("A2", "X123"), Z_RING, ("CB3",)),
    ("f1", ("n1",), Z_RING, ()),
    ("CB1", ("B1",), CORE, ("M0", "O0")),
    ("CQ1", ("Q1",), CORE, ()),
    ("CB2", ("B2",), CORE, ("Q2",)),
    ("CQ2", ("Q2",), CORE, ("f1", "c1")),
    ("CP3", ("P3",), CORE, ("M0", "A2")),
    ("M1", (1, 3,), 1, ()),
    ("M2", (2,), 10, ()),
)
GROUPS = (
    ("k0", "O0", "A1", "A3"),
    ("A2", "X123"),
)
WHERE = {
    (0, 0): (0, 0),
    (0, 1): (0, 1),
    (1, 0): (0, 2),
    (1, 1): (1, 1),
    (2, 0): (1, 0),
    (2, 1): (1, 3),
    (3, 0): (0, 3),
    (3, 1): (1, 2),
}
ROWS = (
    (("b0",), ("P0",), ("Cb0",), ("CP0",)),
    (("B1",), ("Q1",), ("CB1",), ("CQ1",)),
    (("B2",), ("Q2",), ("CB2",), ("CQ2",)),
    (("B3",), ("P3",), ("CB3",), ("CP3",)),
)


def kernel(tile, places, n_a, n_b, has_acc, place_ref, *refs):
    a_refs, b_refs = refs[:n_a], refs[n_a : n_a + n_b]
    refs = refs[n_a + n_b :]
    acc_ref = refs[0] if has_acc else None
    out_ref, lhs, sems = refs[has_acc:]
    first = pl.program_id(0) == 0

    def copies(top):
        rows = pl.ds(top, SPAN)
        return [
            pltpu.make_async_copy(
                a_refs[array].at[part, rows], lhs.at[place_ref[i], rows], sems.at[i, top // SPAN]
            )
            for i, (array, part) in enumerate(places)
        ]

    @pl.when(first)
    def _():
        for top in range(0, 1024, SPAN):
            for copy in copies(top):
                copy.start()

    rhs = jnp.concatenate([ref[...].reshape(-1, tile) for ref in b_refs], axis=0)
    for top in range(0, 1024, SPAN):

        @pl.when(first)
        def _():
            for copy in copies(top):
                copy.wait()

        for at in range(top, top + SPAN, 256):
            rows = slice(at, at + 256)
            left = jnp.concatenate([lhs[i, rows, :] for i in range(rhs.shape[0] // 128)], axis=1)
            total = jnp.dot(left, rhs, preferred_element_type=jnp.float32)
            if has_acc:
                total += acc_ref[rows, :].astype(jnp.float32)
            out_ref[rows, :] = total.astype(out_ref.dtype)


def multiply(acc, pieces, slots, n_slots, b_arrays, weight):
    arrays, places = [], []
    for array, part in pieces:
        at = next((i for i, other in enumerate(arrays) if other is array), None)
        if at is None:
            at = len(arrays)
            arrays.append(array)
        places.append((at, part))
    n_a, n_b, has_acc = len(arrays), len(b_arrays), int(acc is not None)
    depth = sum(b.shape[0] * b.shape[1] for b in b_arrays)
    tile = 512 if depth < 3000 else 256
    anywhere = pl.BlockSpec(memory_space=pl.ANY)
    columns = pl.BlockSpec((1024, tile), lambda j, *_: (0, j))
    return pl.pallas_call(
        functools.partial(kernel, tile, tuple(places), n_a, n_b, has_acc),
        grid_spec=pltpu.PrefetchScalarGridSpec(
            num_scalar_prefetch=1,
            grid=(2048 // tile,),
            in_specs=[anywhere] * n_a
            + [pl.BlockSpec((*b.shape[:2], tile), lambda j, *_: (0, 0, j)) for b in b_arrays]
            + [columns] * has_acc,
            out_specs=columns,
            scratch_shapes=[
                pltpu.VMEM((n_slots, 1024, 128), jnp.bfloat16),
                pltpu.SemaphoreType.DMA((len(places), 1024 // SPAN)),
            ],
        ),
        out_shape=jax.ShapeDtypeStruct((1024, 2048), jnp.bfloat16),
        compiler_params=pltpu.CompilerParams(vmem_limit_bytes=50 * 2**20),
        cost_estimate=pl.CostEstimate(
            flops=int(2 * 1024 * depth * 2048 * weight),
            bytes_accessed=int(20 * 2**20 * weight),
            transcendentals=0,
        ),
    )(jnp.stack(slots).astype(jnp.int32), *arrays, *b_arrays, *([acc] * has_acc))


def local(t2_slab, lambda_block):
    y, row, col = (lax.axis_index(a) for a in AXES)
    xh, c, xl, z = row // 2, row % 2, col // 4, col % 4
    sgn = 2 * c - 1

    def block(layer):
        return lax.dynamic_slice(t2_slab, (lax.rem(layer + 8, 4) * 1024, 0), (1024, 128))[None]

    held = {"k0": block(y), "k1": block(y - sgn), "k3": block(y + sgn), "k2": block(y + 2)}
    held["b0"] = lambda_block[None]
    joined = {}

    def join(names):
        if names not in joined:
            blocks = [held[name] for name in names]
            joined[names] = blocks[0] if len(blocks) == 1 else jnp.concatenate(blocks)
        return joined[names]

    def product(acc, distances, weight):
        base = {s: 8 * i for i, s in enumerate(distances)}
        spare, spared = 8 * len(distances), False
        pieces, slots = [], []
        for t in sorted({t for s in distances for t in (s, -s % 4)}):
            mine, theirs = base.get(t, spare), base.get(-t % 4, spare)
            spared |= spare in (mine, theirs)
            for other in (0, 1):
                group, part = WHERE[t, other]
                steps = [join(GROUPS[group])] + [held[f"{step}{group}"] for step in "nfc"]
                for r in range(4):
                    zz = lax.rem(z + r * sgn + 8, 4)
                    away = jnp.abs(zz // 2 - c)
                    apart = jnp.abs(jnp.abs(xl - other) - xh)
                    pieces.append((steps[r], part))
                    slots.append(mine + away * (theirs - mine) + away * 4 + apart * 2 + zz % 2)
        b_arrays = [join(names) for s in distances for names in ROWS[s]]
        return multiply(acc, pieces, slots, spare + 8 * spared, b_arrays, weight)

    acc = None
    for name, what, how, wait in STEPS:
        if isinstance(how, list):
            sent = join(what)
            if wait:
                sent = lax.optimization_barrier((sent, *(held[other] for other in wait)))[0]
            held[name] = lax.ppermute(sent, AXES, how)
        else:
            acc = held[name] = product(acc, what, how)
    return acc


def solution(mesh):
    placed = (P("row", ("layer", "col")), P(("layer", "row"), "col"))
    return jax.shard_map(
        local, mesh=mesh, in_specs=placed, out_specs=P(("row", "layer"), "col"), check_vma=False
    )
```

time: 329 us -> 124 us (0.38)
  waiting for transfers between devices: 293 us -> 41.3 us
  starting transfers between devices: 0.08 us -> 39.3 us
  Pallas kernels: 0 us -> 39 us
  matrix products: 23.5 us -> 0 us
  between operations: 13.1 us -> 0.28 us
  local copies, waits for them, and re-layouts: 0 us -> 4.02 us
    reduce_scatter x1 -> x0, waiting for transfers between devices: 152 us -> none  [local(): lax.psum_scatter(jnp.dot(amplitude, lambda_layer, preferred_element_type=...]
    all_gather x2 -> x0, waiting for transfers between devices: 139 us -> none  [the longest x1 96 us: local(): amplitude = lax.all_gather(t2_slab, 'col', axis=1, tiled=True)]
    ppermute x0 -> x26, waiting for transfers between devices: none -> 41.3 us  [local(): held[name] = lax.ppermute(sent, AXES, how)]
    ppermute x0 -> x26, starting transfers between devices: none -> 39.3 us  [local(): held[name] = lax.ppermute(sent, AXES, how)]
    pallas_call x0 -> x3, Pallas kernels: none -> 39 us  [multiply(): pl.pallas_call(functools.partial(kernel, tile, tuple(places), n_a, n_b, h...]
    dot_general x1 -> x0, matrix products: 23.5 us -> none  [local(): jnp.dot(amplitude, lambda_layer, preferred_element_type=jnp.float32)]
  transfers between devices with their start and end apart: 3 -> 26, of which waited for: 3 -> 11; matrix products, arithmetic and copies ran while one was open for 0% -> 2% of each run, Pallas kernels for 0% -> 23%
where the time goes in v2:
time: 124 us
  waiting for transfers between devices  41.3 us (33%)
  starting transfers between devices  39.3 us (32%)
  Pallas kernels  39 us (31%)
  local copies, waits for them, and re-layouts  4.02 us (3%)
    ppermute x26, waiting for transfers between devices, local(): held[name] = lax.ppermute(sent, AXES, how)  41.3 us
    ppermute x26, starting transfers between devices, local(): held[name] = lax.ppermute(sent, AXES, how)  39.3 us
    pallas_call x3, Pallas kernels, multiply(): pl.pallas_call(functools.partial(kernel, tile, tuple(places), n_a, n_b, h...  39 us
  transfers between devices with their start and end apart: 26, of which 11 were waited for; matrix products, arithmetic and copies ran while one was open for 2% of the time, Pallas kernels for 23%

profile of v2, /device:TPU:1, one launch (start us, length us, event | category | flops | bytes accessed | tf_op | source)
XLA Modules:
  0.0 124.1 jit_solution(2790318557968584822)
XLA Ops:
  0.0 1.3 %dynamic-slice_bitcast_fusion = (bf16[1,1024,128]{2,1,0:T(8,128)(2,1)S(1)}, bf16[1,1024,128]{2,1,0:T(8,128)(2,1)S(1)}, bf16[1,1024,128]{2,1,0:T(8,128)(2,1)S(1)}, bf16[1,1024,128]{2,1,0:T(8,128)(2,1)S(1)}) fusion(bf16[4096,128]{1,0:T(8,128)(2,1)} %param.2, s32[]{:T(128)S(6)} %select_n.157, s32[]{:T(128)S(6)} %select_n.155, s32[]{:T(128)S(6)} %select_n.154, ...), kind=kLoop, calls=%fused_computation.2 | loop fusion | bytes 2097168 | tf_op jit(solution)/shard_map/broadcast_in_dim | solution.py:173
  1.3 3.6 %collective-permute-start.1 = (bf16[1,1024,128]{2,1,0:T(8,128)(2,1)S(1)}, bf16[1,1024,128]{2,1,0:T(8,128)(2,1)S(1)}, u32[]{:S(2)}, u32[]{:S(2)}) collective-permute-start(bf16[1,1024,128]{2,1,0:T(8,128)(2,1)S(1)} %get-tuple-element.22), channel_id=1, source_target_pairs={{0,32},{1,33},{2,34},{3,35},{4,36},{5,37},{6,38},{7,39},{8,104},{9... | collective-permute-start | bytes 786440 | tf_op jit(solution)/shard_map/ppermute | solution.py:210
  4.9 1.2 collective-permute-start.12
  6.1 0.0 collective-permute-start.2
  6.1 0.0 collective-permute-start.4
  6.1 2.5 %collective-permute-start.11 = (bf16[1,256,2048]{2,1,0:T(8,128)(2,1)}, bf16[1,256,2048]{2,1,0:T(8,128)(2,1)S(1)}, u32[]{:S(2)}, u32[]{:S(2)}) collective-permute-start(bf16[1,256,2048]{2,1,0:T(8,128)(2,1)} %bitcast.11.refs_4_), channel_id=1, source_target_pairs={{0,16},{1,17},{2,18},{3,19},{4,20},{5,21},{6,22},{7,23},{8,24},{9,... | collective-permute-start | bytes 3145736 | tf_op jit(solution)/shard_map/ppermute | solution.py:210
  8.6 0.0 collective-permute-done.1
  8.6 3.8 %collective-permute-start = (bf16[1,1024,128]{2,1,0:T(8,128)(2,1)S(1)}, bf16[1,1024,128]{2,1,0:T(8,128)(2,1)S(1)}, u32[]{:S(2)}, u32[]{:S(2)}) collective-permute-start(bf16[1,1024,128]{2,1,0:T(8,128)(2,1)S(1)} %get-tuple-element.23), channel_id=1, source_target_pairs={{0,64},{1,65},{2,66},{3,67},{4,68},{5,69},{6,70},{7,71},{8,72},{9,... | collective-permute-start | bytes 786440 | tf_op jit(solution)/shard_map/ppermute | solution.py:210
  12.4 0.9 collective-permute-done.12
  13.3 0.0 collective-permute-done.2
  13.3 0.1 pad_maximum_fusion.refs_0_
  13.5 3.8 %collective-permute-start.15 = (bf16[4,1024,128]{2,1,0:T(8,128)(2,1)S(1)}, bf16[4,1024,128]{2,1,0:T(8,128)(2,1)S(1)}, u32[]{:S(2)}, u32[]{:S(2)}) collective-permute-start(bf16[4,1024,128]{2,1,0:T(8,128)(2,1)S(1)} %pad_maximum_fusion.refs_0_), channel_id=1, source_target_pairs={{0,1},{1,2},{2,3},{3,0},{4,5},{5,6},{6,7},{7,4},{8,11},{9,8},{10,9... | collective-permute-start | bytes 3145736 | tf_op jit(solution)/shard_map/ppermute | solution.py:210
  17.3 0.0 collective-permute-start.13
  17.3 13.7 %collective-permute-done = bf16[1,1024,128]{2,1,0:T(8,128)(2,1)S(1)} collective-permute-done((bf16[1,1024,128]{2,1,0:T(8,128)(2,1)S(1)}, bf16[1,1024,128]{2,1,0:T(8,128)(2,1)S(1)}, u32[]{:S(2)}, u32[]{:S(2)}) %collective-permute-start) | collective-permute-done | bytes 262176 | tf_op jit(solution)/shard_map/ppermute | solution.py:210
  30.9 0.1 pad_maximum_fusion.1
  31.0 0.6 collective-permute-start.3
  31.6 0.0 collective-permute-done.4.refs_12_
  31.6 0.0 collective-permute-start.5
  31.6 6.2 %collective-permute-done.11.refs_5_ = bf16[1,256,2048]{2,1,0:T(8,128)(2,1)S(1)} collective-permute-done((bf16[1,256,2048]{2,1,0:T(8,128)(2,1)}, bf16[1,256,2048]{2,1,0:T(8,128)(2,1)S(1)}, u32[]{:S(2)}, u32[]{:S(2)}) %collective-permute-start.11) | collective-permute-done | bytes 1048608 | tf_op jit(solution)/shard_map/ppermute | solution.py:210
  37.8 0.0 collective-permute-start.9
  37.8 0.1 collective-permute-done.15.refs_1_
  38.0 3.7 %collective-permute-start.16 = (bf16[4,1024,128]{2,1,0:T(8,128)(2,1)S(1)}, bf16[4,1024,128]{2,1,0:T(8,128)(2,1)S(1)}, u32[]{:S(2)}, u32[]{:S(2)}) collective-permute-start(bf16[4,1024,128]{2,1,0:T(8,128)(2,1)S(1)} %collective-permute-done.15.refs_1_), channel_id=1, source_target_pairs={{0,1},{1,2},{2,3},{3,0},{4,5},{5,6},{6,7},{7,4},{8,11},{9,8},{10,9... | collective-permute-start | bytes 3145736 | tf_op jit(solution)/shard_map/ppermute | solution.py:210
  41.7 1.3 %collective-permute-done.13.refs_3_ = bf16[4,1024,128]{2,1,0:T(8,128)(2,1)S(1)} collective-permute-done((bf16[4,1024,128]{2,1,0:T(8,128)(2,1)S(1)}, bf16[4,1024,128]{2,1,0:T(8,128)(2,1)S(1)}, u32[]{:S(2)}, u32[]{:S(2)}) %collective-permute-start.13) | collective-permute-done | bytes 1048608 | tf_op jit(solution)/shard_map/ppermute | solution.py:210
  42.9 0.6 collective-permute-start.14
  43.6 8.5 %collective-permute-done.3 = bf16[3,1024,128]{2,1,0:T(8,128)(2,1)S(1)} collective-permute-done((bf16[3,1024,128]{2,1,0:T(8,128)(2,1)S(1)}, bf16[3,1024,128]{2,1,0:T(8,128)(2,1)S(1)}, u32[]{:S(2)}, u32[]{:S(2)}) %collective-permute-start.3) | collective-permute-done | bytes 786464 | tf_op jit(solution)/shard_map/ppermute | solution.py:210
  52.1 0.8 collective-permute-start.20
  52.9 0.7 constant_dynamic-update-slice_fusion.1
  53.6 1.0 constant_dynamic-update-slice_fusion.refs_4_.refs_0_
  54.6 0.0 collective-permute-done.5.refs_14_
  54.6 0.0 collective-permute-start.21
  54.6 0.0 collective-permute-done.9.refs_8_
  54.6 3.8 %collective-permute-start.6 = (bf16[4,1024,128]{2,1,0:T(8,128)(2,1)}, bf16[4,1024,128]{2,1,0:T(8,128)(2,1)}, u32[]{:S(2)}, u32[]{:S(2)}) collective-permute-start(bf16[4,1024,128]{2,1,0:T(8,128)(2,1)} %constant_dynamic-update-slice_fusion.refs_4_.refs_0_), channel_id=1, source_target_pairs={{0,1},{1,2},{2,3},{3,0},{4,5},{5,6},{6,7},{7,4},{8,11},{9,8},{10,9... | collective-permute-start | bytes 3145736 | tf_op jit(solution)/shard_map/ppermute | solution.py:210
  58.5 0.0 collective-permute-done.16.refs_2_
  58.5 0.0 copy-done
  58.5 2.9 %collective-permute-start.24 = (bf16[1,256,2048]{2,1,0:T(8,128)(2,1)}, bf16[1,256,2048]{2,1,0:T(8,128)(2,1)}, u32[]{:S(2)}, u32[]{:S(2)}) collective-permute-start(bf16[1,256,2048]{2,1,0:T(8,128)(2,1)} %collective-permute-done.4.refs_12_), channel_id=1, source_target_pairs={{0,16},{1,17},{2,18},{3,19},{4,20},{5,21},{6,22},{7,23},{8,24},{9,... | collective-permute-start | bytes 3145736 | tf_op jit(solution)/shard_map/ppermute | solution.py:210
  61.4 2.0 %collective-permute-done.14.refs_9_ = bf16[1,256,2048]{2,1,0:T(8,128)(2,1)} collective-permute-done((bf16[1,256,2048]{2,1,0:T(8,128)(2,1)S(1)}, bf16[1,256,2048]{2,1,0:T(8,128)(2,1)}, u32[]{:S(2)}, u32[]{:S(2)}) %collective-permute-start.14) | collective-permute-done | bytes 1048608 | tf_op jit(solution)/shard_map/ppermute | solution.py:210
  63.3 1.2 collective-permute-start.10
  64.6 0.0 collective-permute-done.20.refs_6_
  64.6 0.1 collective-permute-start.17
  64.6 0.0 collective-permute-done.21.refs_7_
  64.6 0.9 copy-done.2
  65.5 1.6 %collective-permute-start.8 = (bf16[4,1024,128]{2,1,0:T(8,128)(2,1)}, bf16[4,1024,128]{2,1,0:T(8,128)(2,1)}, u32[]{:S(2)}, u32[]{:S(2)}) collective-permute-start(bf16[4,1024,128]{2,1,0:T(8,128)(2,1)} %constant_dynamic-update-slice_fusion.refs_4_.refs_0_), channel_id=1, source_target_pairs={{0,3},{1,0},{2,1},{3,2},{4,7},{5,4},{6,5},{7,6},{8,9},{9,10},{10,1... | collective-permute-start | bytes 3145736 | tf_op jit(solution)/shard_map/ppermute | solution.py:210
  67.2 3.4 %collective-permute-done.6.refs_5_.refs_1_ = bf16[4,1024,128]{2,1,0:T(8,128)(2,1)} collective-permute-done((bf16[4,1024,128]{2,1,0:T(8,128)(2,1)}, bf16[4,1024,128]{2,1,0:T(8,128)(2,1)}, u32[]{:S(2)}, u32[]{:S(2)}) %collective-permute-start.6) | collective-permute-done | bytes 1048608 | tf_op jit(solution)/shard_map/ppermute | solution.py:210
  70.5 3.4 %collective-permute-start.7 = (bf16[4,1024,128]{2,1,0:T(8,128)(2,1)}, bf16[4,1024,128]{2,1,0:T(8,128)(2,1)}, u32[]{:S(2)}, u32[]{:S(2)}) collective-permute-start(bf16[4,1024,128]{2,1,0:T(8,128)(2,1)} %collective-permute-done.6.refs_5_.refs_1_), channel_id=1, source_target_pairs={{0,1},{1,2},{2,3},{3,0},{4,5},{5,6},{6,7},{7,4},{8,11},{9,8},{10,9... | collective-permute-start | bytes 3145736 | tf_op jit(solution)/shard_map/ppermute | solution.py:210
  73.9 0.1 stack.95.place_ref
  74.0 11.1 %shard_map.28.refs_16_ = bf16[1024,2048]{1,0:T(8,128)(2,1)} custom-call(s32[8]{0:T(128)S(1)} %stack.95.place_ref, bf16[4,1024,128]{2,1,0:T(8,128)(2,1)S(1)} %pad_maximum_fusion.refs_0_, bf16[4,1024,128]{2,1,0:T(8,128)(2,1)S(1)} %collective-permute-done.15.refs_1_, bf16[4,1024,128]{2,1,0:T(8,128)(2,1)S(1)} %collective-permute-done.16.refs_2_, ...), custom_call_target="tpu_custom_call" | custom-call | flops 42949672 | bytes 209715 | tf_op jit(solution)/shard_map/pallas_call | solution.py:143
  85.1 0.0 collective-permute-done.24.refs_13_
  85.1 0.7 collective-permute-start.25
  85.9 0.0 collective-permute-done.10.refs_4_
  85.9 0.0 collective-permute-start.22
  85.9 3.0 %collective-permute-done.17.refs_5_ = bf16[1,256,2048]{2,1,0:T(8,128)(2,1)} collective-permute-done((bf16[1,256,2048]{2,1,0:T(8,128)(2,1)}, bf16[1,256,2048]{2,1,0:T(8,128)(2,1)}, u32[]{:S(2)}, u32[]{:S(2)}) %collective-permute-start.17) | collective-permute-done | bytes 1048608 | tf_op jit(solution)/shard_map/ppermute | solution.py:210
  88.8 4.5 %collective-permute-start.23 = (bf16[1,256,2048]{2,1,0:T(8,128)(2,1)}, bf16[1,256,2048]{2,1,0:T(8,128)(2,1)}, u32[]{:S(2)}, u32[]{:S(2)}) collective-permute-start(bf16[1,256,2048]{2,1,0:T(8,128)(2,1)} %collective-permute-done.14.refs_9_), channel_id=1, source_target_pairs={{0,8},{1,9},{2,10},{3,11},{4,12},{5,13},{6,14},{7,15},{8,0},{9,1},... | collective-permute-start | bytes 3145736 | tf_op jit(solution)/shard_map/ppermute | solution.py:210
  93.4 0.0 collective-permute-done.8.refs_7_.refs_3_
  93.4 0.0 collective-permute-start.18
  93.4 1.1 collective-permute-done.7.refs_6_.refs_2_
  94.5 0.3 collective-permute-start.19
  94.7 0.1 stack.112.place_ref
  94.8 0.0 collective-permute-done.25.refs_15_
  94.8 0.0 collective-permute-done.22.refs_10_
  94.8 1.1 collective-permute-done.23.refs_11_
  96.0 16.8 %shard_map.29.refs_8_ = bf16[1024,2048]{1,0:T(8,128)(2,1)} custom-call(s32[16]{0:T(128)S(1)} %stack.112.place_ref, bf16[4,1024,128]{2,1,0:T(8,128)(2,1)S(1)} %pad_maximum_fusion.refs_0_, bf16[4,1024,128]{2,1,0:T(8,128)(2,1)S(1)} %collective-permute-done.15.refs_1_, bf16[4,1024,128]{2,1,0:T(8,128)(2,1)S(1)} %collective-permute-done.16.refs_2_, ...), custom_call_target="tpu_custom_call" | custom-call | flops 8589934592 | bytes 20971520 | tf_op jit(solution)/shard_map/pallas_call | solution.py:143
  112.8 0.0 collective-permute-done.18.refs_6_
  112.9 0.0 collective-permute-done.19.refs_7_
  112.9 11.1 %shard_map.30 = bf16[1024,2048]{1,0:T(8,128)(2,1)} custom-call(s32[8]{0:T(128)S(1)} %stack.95.place_ref, bf16[4,1024,128]{2,1,0:T(8,128)(2,1)} %constant_dynamic-update-slice_fusion.refs_4_.refs_0_, bf16[4,1024,128]{2,1,0:T(8,128)(2,1)} %collective-permute-done.6.refs_5_.refs_1_, bf16[4,1024,128]{2,1,0:T(8,128)(2,1)} %collective-permute-done.7.refs_6_.refs_2_, ...), custom_call_target="tpu_custom_call" | custom-call | flops 42949672960 | bytes 209715200 | tf_op jit(solution)/shard_map/pallas_call | solution.py:143
  (8 shorter events, 0.0 us)
Async XLA Ops:
  1.3 7.3 %collective-permute-start.1 = (bf16[1,1024,128]{2,1,0:T(8,128)(2,1)S(1)}, bf16[1,1024,128]{2,1,0:T(8,128)(2,1)S(1)}, u32[]{:S(2)}, u32[]{:S(2)}) collective-permute-start(bf16[1,1024,128]{2,1,0:T(8,128)(2,1)S(1)} %get-tuple-element.22), channel_id=1, source_target_pairs={{0,32},{1,33},{2,34},{3,35},{4,36},{5,37},{6,38},{7,39},{8,104},{9... | collective-permute-start | bytes 786440 | tf_op jit(solution)/shard_map/ppermute | solution.py:210
  4.9 8.4 %collective-permute-start.12 = (bf16[1,1024,128]{2,1,0:T(8,128)(2,1)S(1)}, bf16[1,1024,128]{2,1,0:T(8,128)(2,1)S(1)}, u32[]{:S(2)}, u32[]{:S(2)}) collective-permute-start(bf16[1,1024,128]{2,1,0:T(8,128)(2,1)S(1)} %get-tuple-element.21), channel_id=1, source_target_pairs={{0,4},{1,5},{2,6},{3,7},{4,0},{5,1},{6,2},{7,3},{8,12},{9,13},{10,... | collective-permute-start | bytes 786440 | tf_op jit(solution)/shard_map/ppermute | solution.py:210
  6.1 7.2 %collective-permute-start.2 = (bf16[1,1024,128]{2,1,0:T(8,128)(2,1)S(1)}, bf16[1,1024,128]{2,1,0:T(8,128)(2,1)S(1)}, u32[]{:S(2)}, u32[]{:S(2)}) collective-permute-start(bf16[1,1024,128]{2,1,0:T(8,128)(2,1)S(1)} %get-tuple-element.24), channel_id=1, source_target_pairs={{0,96},{1,97},{2,98},{3,99},{4,100},{5,101},{6,102},{7,103},{8,40}... | collective-permute-start | bytes 786440 | tf_op jit(solution)/shard_map/ppermute | solution.py:210
  6.1 25.5 %collective-permute-start.4 = (bf16[1,256,2048]{2,1,0:T(8,128)(2,1)}, bf16[1,256,2048]{2,1,0:T(8,128)(2,1)}, u32[]{:S(2)}, u32[]{:S(2)}) collective-permute-start(bf16[1,256,2048]{2,1,0:T(8,128)(2,1)} %bitcast.11.refs_4_), channel_id=1, source_target_pairs={{0,96},{1,97},{2,98},{3,99},{4,100},{5,101},{6,102},{7,103},{8,40}... | collective-permute-start | bytes 3145736 | tf_op jit(solution)/shard_map/ppermute | solution.py:210
  6.1 31.7 %collective-permute-start.11 = (bf16[1,256,2048]{2,1,0:T(8,128)(2,1)}, bf16[1,256,2048]{2,1,0:T(8,128)(2,1)S(1)}, u32[]{:S(2)}, u32[]{:S(2)}) collective-permute-start(bf16[1,256,2048]{2,1,0:T(8,128)(2,1)} %bitcast.11.refs_4_), channel_id=1, source_target_pairs={{0,16},{1,17},{2,18},{3,19},{4,20},{5,21},{6,22},{7,23},{8,24},{9,... | collective-permute-start | bytes 3145736 | tf_op jit(solution)/shard_map/ppermute | solution.py:210
  8.6 22.3 %collective-permute-start = (bf16[1,1024,128]{2,1,0:T(8,128)(2,1)S(1)}, bf16[1,1024,128]{2,1,0:T(8,128)(2,1)S(1)}, u32[]{:S(2)}, u32[]{:S(2)}) collective-permute-start(bf16[1,1024,128]{2,1,0:T(8,128)(2,1)S(1)} %get-tuple-element.23), channel_id=1, source_target_pairs={{0,64},{1,65},{2,66},{3,67},{4,68},{5,69},{6,70},{7,71},{8,72},{9,... | collective-permute-start | bytes 786440 | tf_op jit(solution)/shard_map/ppermute | solution.py:210
  13.5 24.5 %collective-permute-start.15 = (bf16[4,1024,128]{2,1,0:T(8,128)(2,1)S(1)}, bf16[4,1024,128]{2,1,0:T(8,128)(2,1)S(1)}, u32[]{:S(2)}, u32[]{:S(2)}) collective-permute-start(bf16[4,1024,128]{2,1,0:T(8,128)(2,1)S(1)} %pad_maximum_fusion.refs_0_), channel_id=1, source_target_pairs={{0,1},{1,2},{2,3},{3,0},{4,5},{5,6},{6,7},{7,4},{8,11},{9,8},{10,9... | collective-permute-start | bytes 3145736 | tf_op jit(solution)/shard_map/ppermute | solution.py:210
  17.3 25.7 %collective-permute-start.13 = (bf16[4,1024,128]{2,1,0:T(8,128)(2,1)S(1)}, bf16[4,1024,128]{2,1,0:T(8,128)(2,1)S(1)}, u32[]{:S(2)}, u32[]{:S(2)}) collective-permute-start(bf16[4,1024,128]{2,1,0:T(8,128)(2,1)S(1)} %pad_maximum_fusion.refs_0_), channel_id=1, source_target_pairs={{0,3},{1,0},{2,1},{3,2},{4,7},{5,4},{6,5},{7,6},{8,9},{9,10},{10,1... | collective-permute-start | bytes 3145736 | tf_op jit(solution)/shard_map/ppermute | solution.py:210
  31.0 21.1 %collective-permute-start.3 = (bf16[3,1024,128]{2,1,0:T(8,128)(2,1)S(1)}, bf16[3,1024,128]{2,1,0:T(8,128)(2,1)S(1)}, u32[]{:S(2)}, u32[]{:S(2)}) collective-permute-start(bf16[3,1024,128]{2,1,0:T(8,128)(2,1)S(1)} %pad_maximum_fusion.1), channel_id=1, source_target_pairs={{0,4},{1,5},{2,6},{3,7},{4,0},{5,1},{6,2},{7,3},{8,12},{9,13},{10,... | collective-permute-start | bytes 2359304 | tf_op jit(solution)/shard_map/ppermute | solution.py:210
  31.6 23.0 %collective-permute-start.5 = (bf16[1,256,2048]{2,1,0:T(8,128)(2,1)}, bf16[1,256,2048]{2,1,0:T(8,128)(2,1)S(1)}, u32[]{:S(2)}, u32[]{:S(2)}) collective-permute-start(bf16[1,256,2048]{2,1,0:T(8,128)(2,1)} %collective-permute-done.4.refs_12_), channel_id=1, source_target_pairs={{0,8},{1,9},{2,10},{3,11},{4,12},{5,13},{6,14},{7,15},{8,0},{9,1},... | collective-permute-start | bytes 3145736 | tf_op jit(solution)/shard_map/ppermute | solution.py:210
  37.8 23.5 %copy-start.1 = (bf16[1,256,2048]{2,1,0:T(8,128)(2,1)}, bf16[1,256,2048]{2,1,0:T(8,128)(2,1)S(1)}, u32[]{:S(2)}) copy-start(bf16[1,256,2048]{2,1,0:T(8,128)(2,1)S(1)} %collective-permute-done.11.refs_5_) | copy-start | bytes 3145732
  37.8 16.8 %collective-permute-start.9 = (bf16[1,256,2048]{2,1,0:T(8,128)(2,1)}, bf16[1,256,2048]{2,1,0:T(8,128)(2,1)}, u32[]{:S(2)}, u32[]{:S(2)}) collective-permute-start(bf16[1,256,2048]{2,1,0:T(8,128)(2,1)} %bitcast.11.refs_4_), channel_id=1, source_target_pairs={{0,32},{1,33},{2,34},{3,35},{4,36},{5,37},{6,38},{7,39},{8,104},{9... | collective-permute-start | bytes 3145736 | tf_op jit(solution)/shard_map/ppermute | solution.py:210
  38.0 20.5 %collective-permute-start.16 = (bf16[4,1024,128]{2,1,0:T(8,128)(2,1)S(1)}, bf16[4,1024,128]{2,1,0:T(8,128)(2,1)S(1)}, u32[]{:S(2)}, u32[]{:S(2)}) collective-permute-start(bf16[4,1024,128]{2,1,0:T(8,128)(2,1)S(1)} %collective-permute-done.15.refs_1_), channel_id=1, source_target_pairs={{0,1},{1,2},{2,3},{3,0},{4,5},{5,6},{6,7},{7,4},{8,11},{9,8},{10,9... | collective-permute-start | bytes 3145736 | tf_op jit(solution)/shard_map/ppermute | solution.py:210
  42.9 15.5 %copy-start = (bf16[4,1024,128]{2,1,0:T(8,128)(2,1)}, bf16[4,1024,128]{2,1,0:T(8,128)(2,1)S(1)}, u32[]{:S(2)}) copy-start(bf16[4,1024,128]{2,1,0:T(8,128)(2,1)S(1)} %collective-permute-done.13.refs_3_) | copy-start | bytes 3145732
  42.9 20.4 %collective-permute-start.14 = (bf16[1,256,2048]{2,1,0:T(8,128)(2,1)S(1)}, bf16[1,256,2048]{2,1,0:T(8,128)(2,1)}, u32[]{:S(2)}, u32[]{:S(2)}) collective-permute-start(bf16[1,256,2048]{2,1,0:T(8,128)(2,1)S(1)} %collective-permute-done.11.refs_5_), channel_id=1, source_target_pairs={{0,32},{1,33},{2,34},{3,35},{4,36},{5,37},{6,38},{7,39},{8,104},{9... | collective-permute-start | bytes 3145736 | tf_op jit(solution)/shard_map/ppermute | solution.py:210
  52.1 12.5 %collective-permute-start.20 = (bf16[1,256,2048]{2,1,0:T(8,128)(2,1)}, bf16[1,256,2048]{2,1,0:T(8,128)(2,1)S(1)}, u32[]{:S(2)}, u32[]{:S(2)}) collective-permute-start(bf16[1,256,2048]{2,1,0:T(8,128)(2,1)} %bitcast.11.refs_4_), channel_id=1, source_target_pairs={{0,8},{1,9},{2,10},{3,11},{4,12},{5,13},{6,14},{7,15},{8,0},{9,1},... | collective-permute-start | bytes 3145736 | tf_op jit(solution)/shard_map/ppermute | solution.py:210
  54.6 15.9 %copy-start.4 = (bf16[1,256,2048]{2,1,0:T(8,128)(2,1)}, bf16[1,256,2048]{2,1,0:T(8,128)(2,1)S(1)}, u32[]{:S(2)}) copy-start(bf16[1,256,2048]{2,1,0:T(8,128)(2,1)S(1)} %collective-permute-done.5.refs_14_) | copy-start | bytes 3145732
  54.6 10.0 %collective-permute-start.21 = (bf16[1,256,2048]{2,1,0:T(8,128)(2,1)S(1)}, bf16[1,256,2048]{2,1,0:T(8,128)(2,1)S(1)}, u32[]{:S(2)}, u32[]{:S(2)}) collective-permute-start(bf16[1,256,2048]{2,1,0:T(8,128)(2,1)S(1)} %collective-permute-done.11.refs_5_), channel_id=1, source_target_pairs={{0,8},{1,9},{2,10},{3,11},{4,12},{5,13},{6,14},{7,15},{8,0},{9,1},... | collective-permute-start | bytes 3145736 | tf_op jit(solution)/shard_map/ppermute | solution.py:210
  54.6 15.9 %collective-permute-start.6 = (bf16[4,1024,128]{2,1,0:T(8,128)(2,1)}, bf16[4,1024,128]{2,1,0:T(8,128)(2,1)}, u32[]{:S(2)}, u32[]{:S(2)}) collective-permute-start(bf16[4,1024,128]{2,1,0:T(8,128)(2,1)} %constant_dynamic-update-slice_fusion.refs_4_.refs_0_), channel_id=1, source_target_pairs={{0,1},{1,2},{2,3},{3,0},{4,5},{5,6},{6,7},{7,4},{8,11},{9,8},{10,9... | collective-permute-start | bytes 3145736 | tf_op jit(solution)/shard_map/ppermute | solution.py:210
  58.5 26.7 %collective-permute-start.24 = (bf16[1,256,2048]{2,1,0:T(8,128)(2,1)}, bf16[1,256,2048]{2,1,0:T(8,128)(2,1)}, u32[]{:S(2)}, u32[]{:S(2)}) collective-permute-start(bf16[1,256,2048]{2,1,0:T(8,128)(2,1)} %collective-permute-done.4.refs_12_), channel_id=1, source_target_pairs={{0,16},{1,17},{2,18},{3,19},{4,20},{5,21},{6,22},{7,23},{8,24},{9,... | collective-permute-start | bytes 3145736 | tf_op jit(solution)/shard_map/ppermute | solution.py:210
  63.3 22.5 %collective-permute-start.10 = (bf16[1,256,2048]{2,1,0:T(8,128)(2,1)}, bf16[1,256,2048]{2,1,0:T(8,128)(2,1)}, u32[]{:S(2)}, u32[]{:S(2)}) collective-permute-start(bf16[1,256,2048]{2,1,0:T(8,128)(2,1)} %collective-permute-done.9.refs_8_), channel_id=1, source_target_pairs={{0,32},{1,33},{2,34},{3,35},{4,36},{5,37},{6,38},{7,39},{8,104},{9... | collective-permute-start | bytes 3145736 | tf_op jit(solution)/shard_map/ppermute | solution.py:210
  64.6 1.0 copy-start.2
  64.6 24.3 %collective-permute-start.17 = (bf16[1,256,2048]{2,1,0:T(8,128)(2,1)}, bf16[1,256,2048]{2,1,0:T(8,128)(2,1)}, u32[]{:S(2)}, u32[]{:S(2)}) collective-permute-start(bf16[1,256,2048]{2,1,0:T(8,128)(2,1)} %collective-permute-done.14.refs_9_), channel_id=1, source_target_pairs={{0,32},{1,33},{2,34},{3,35},{4,36},{5,37},{6,38},{7,39},{8,104},{9... | collective-permute-start | bytes 3145736 | tf_op jit(solution)/shard_map/ppermute | solution.py:210
  65.5 1.6 %copy-start.3 = (bf16[1,256,2048]{2,1,0:T(8,128)(2,1)}, bf16[1,256,2048]{2,1,0:T(8,128)(2,1)S(1)}, u32[]{:S(2)}) copy-start(bf16[1,256,2048]{2,1,0:T(8,128)(2,1)S(1)} %collective-permute-done.21.refs_7_) | copy-start | bytes 3145732
  65.5 27.8 %collective-permute-start.8 = (bf16[4,1024,128]{2,1,0:T(8,128)(2,1)}, bf16[4,1024,128]{2,1,0:T(8,128)(2,1)}, u32[]{:S(2)}, u32[]{:S(2)}) collective-permute-start(bf16[4,1024,128]{2,1,0:T(8,128)(2,1)} %constant_dynamic-update-slice_fusion.refs_4_.refs_0_), channel_id=1, source_target_pairs={{0,3},{1,0},{2,1},{3,2},{4,7},{5,4},{6,5},{7,6},{8,9},{9,10},{10,1... | collective-permute-start | bytes 3145736 | tf_op jit(solution)/shard_map/ppermute | solution.py:210
  70.5 23.9 %collective-permute-start.7 = (bf16[4,1024,128]{2,1,0:T(8,128)(2,1)}, bf16[4,1024,128]{2,1,0:T(8,128)(2,1)}, u32[]{:S(2)}, u32[]{:S(2)}) collective-permute-start(bf16[4,1024,128]{2,1,0:T(8,128)(2,1)} %collective-permute-done.6.refs_5_.refs_1_), channel_id=1, source_target_pairs={{0,1},{1,2},{2,3},{3,0},{4,5},{5,6},{6,7},{7,4},{8,11},{9,8},{10,9... | collective-permute-start | bytes 3145736 | tf_op jit(solution)/shard_map/ppermute | solution.py:210
  85.1 9.7 %collective-permute-start.25 = (bf16[1,256,2048]{2,1,0:T(8,128)(2,1)}, bf16[1,256,2048]{2,1,0:T(8,128)(2,1)}, u32[]{:S(2)}, u32[]{:S(2)}) collective-permute-start(bf16[1,256,2048]{2,1,0:T(8,128)(2,1)} %collective-permute-done.24.refs_13_), channel_id=1, source_target_pairs={{0,8},{1,9},{2,10},{3,11},{4,12},{5,13},{6,14},{7,15},{8,0},{9,1},... | collective-permute-start | bytes 3145736 | tf_op jit(solution)/shard_map/ppermute | solution.py:210
  85.9 9.0 %collective-permute-start.22 = (bf16[1,256,2048]{2,1,0:T(8,128)(2,1)}, bf16[1,256,2048]{2,1,0:T(8,128)(2,1)}, u32[]{:S(2)}, u32[]{:S(2)}) collective-permute-start(bf16[1,256,2048]{2,1,0:T(8,128)(2,1)} %collective-permute-done.9.refs_8_), channel_id=1, source_target_pairs={{0,8},{1,9},{2,10},{3,11},{4,12},{5,13},{6,14},{7,15},{8,0},{9,1},... | collective-permute-start | bytes 3145736 | tf_op jit(solution)/shard_map/ppermute | solution.py:210
  88.8 7.2 %collective-permute-start.23 = (bf16[1,256,2048]{2,1,0:T(8,128)(2,1)}, bf16[1,256,2048]{2,1,0:T(8,128)(2,1)}, u32[]{:S(2)}, u32[]{:S(2)}) collective-permute-start(bf16[1,256,2048]{2,1,0:T(8,128)(2,1)} %collective-permute-done.14.refs_9_), channel_id=1, source_target_pairs={{0,8},{1,9},{2,10},{3,11},{4,12},{5,13},{6,14},{7,15},{8,0},{9,1},... | collective-permute-start | bytes 3145736 | tf_op jit(solution)/shard_map/ppermute | solution.py:210
  93.4 19.5 %collective-permute-start.18 = (bf16[1,256,2048]{2,1,0:T(8,128)(2,1)}, bf16[1,256,2048]{2,1,0:T(8,128)(2,1)}, u32[]{:S(2)}, u32[]{:S(2)}) collective-permute-start(bf16[1,256,2048]{2,1,0:T(8,128)(2,1)} %collective-permute-done.10.refs_4_), channel_id=1, source_target_pairs={{0,8},{1,9},{2,10},{3,11},{4,12},{5,13},{6,14},{7,15},{8,0},{9,1},... | collective-permute-start | bytes 3145736 | tf_op jit(solution)/shard_map/ppermute | solution.py:210
  94.5 18.4 %collective-permute-start.19 = (bf16[1,256,2048]{2,1,0:T(8,128)(2,1)}, bf16[1,256,2048]{2,1,0:T(8,128)(2,1)}, u32[]{:S(2)}, u32[]{:S(2)}) collective-permute-start(bf16[1,256,2048]{2,1,0:T(8,128)(2,1)} %collective-permute-done.17.refs_5_), channel_id=1, source_target_pairs={{0,8},{1,9},{2,10},{3,11},{4,12},{5,13},{6,14},{7,15},{8,0},{9,1},... | collective-permute-start | bytes 3145736 | tf_op jit(solution)/shard_map/ppermute | solution.py:210

commit v3 on v2

--- a/solution.py
+++ b/solution.py
@@ -8,7 +8,7 @@
 from jax.sharding import PartitionSpec as P
 
 AXES = ("layer", "row", "col")
-SPAN = 512
+SPAN = 1024
 
 
 def flat(y, xh, c, xl, z):
@@ -38,33 +38,33 @@
 STEPS = (
     ("A1", ("k1",), Y_RING, ()),
     ("A3", ("k3",), Y_BACK, ()),
-    ("A2", ("k2",), Y_FAR, ()),
     ("O0", ("k0",), XL, ()),
     ("P0", ("b0",), XH, ()),
-    ("X123", ("A1", "A3", "A2"), XL, ()),
     ("B3", ("b0",), Y_BACK, ()),
-    ("B1", ("b0",), Y_RING, ()),
-    ("B2", ("B1",), Y_RING, ()),
     ("n0", ("k0", "O0", "A1", "A3"), Z_RING, ()),
     ("c0", ("k0", "O0", "A1", "A3"), Z_BACK, ()),
     ("f0", ("n0",), Z_RING, ()),
-    ("c1", ("A2", "X123"), Z_BACK, ()),
     ("Cb0", ("b0",), CORE, ()),
     ("CP0", ("P0",), CORE, ()),
     ("CB3", ("B3",), CORE, ()),
     ("M0", (0,), 0.01, ()),
+    ("A2", ("k2",), Y_FAR, ("O0",)),
+    ("X123", ("A1", "A3", "A2"), XL, ()),
+    ("B1", ("b0",), Y_RING, ("A2",)),
+    ("B2", ("B1",), Y_RING, ()),
     ("Q1", ("P0",), Y_RING, ("c0",)),
     ("Q2", ("Q1",), Y_RING, ("f0", "X123", "A2")),
     ("P3", ("B3",), XH, ("n0",)),
     ("n1", ("A2", "X123"), Z_RING, ("CB3",)),
+    ("c1", ("A2", "X123"), Z_BACK, ()),
     ("f1", ("n1",), Z_RING, ()),
-    ("CB1", ("B1",), CORE, ("M0", "O0")),
+    ("CB1", ("B1",), CORE, ("M0",)),
     ("CQ1", ("Q1",), CORE, ()),
-    ("CB2", ("B2",), CORE, ("Q2",)),
+    ("CB2", ("B2",), CORE, ("Q2", "f0", "A2")),
     ("CQ2", ("Q2",), CORE, ("f1", "c1")),
     ("CP3", ("P3",), CORE, ("M0", "A2")),
     ("M1", (1, 3,), 1, ()),
-    ("M2", (2,), 10, ()),
+    ("M2", (2,), 3, ()),
 )
 GROUPS = (
     ("k0", "O0", "A1", "A3"),

time: 124 us -> 121 us (0.976)
  waiting for transfers between devices: 41.3 us -> 35.2 us
  starting transfers between devices: 39.3 us -> 45.2 us
  Pallas kernels: 39 us -> 35.7 us
    ppermute x26, waiting for transfers between devices: 41.3 us -> 35.2 us  [local(): held[name] = lax.ppermute(sent, AXES, how)]
    ppermute x26, starting transfers between devices: 39.3 us -> 45.2 us  [local(): held[name] = lax.ppermute(sent, AXES, how)]
    pallas_call x3, Pallas kernels: 39 us -> 35.7 us  [multiply(): pl.pallas_call(functools.partial(kernel, tile, tuple(places), n_a, n_b, h...]
  transfers between devices with their start and end apart: 26 -> 26, of which waited for: 11 -> 13; matrix products, arithmetic and copies ran while one was open for 2% -> 2% of each run, Pallas kernels for 23% -> 21%
where the time goes in v3:
time: 121 us
  starting transfers between devices  45.2 us (37%)
  Pallas kernels  35.7 us (30%)
  waiting for transfers between devices  35.2 us (29%)
  local copies, waits for them, and re-layouts  4.01 us (3%)
    ppermute x26, starting transfers between devices, local(): held[name] = lax.ppermute(sent, AXES, how)  45.2 us
    pallas_call x3, Pallas kernels, multiply(): pl.pallas_call(functools.partial(kernel, tile, tuple(places), n_a, n_b, h...  35.7 us
    ppermute x26, waiting for transfers between devices, local(): held[name] = lax.ppermute(sent, AXES, how)  35.2 us
  transfers between devices with their start and end apart: 26, of which 13 were waited for; matrix products, arithmetic and copies ran while one was open for 2% of the time, Pallas kernels for 21%

profile of v3, /device:TPU:1, one launch (start us, length us, event | category | flops | bytes accessed | tf_op | source)
XLA Modules:
  0.0 120.7 jit_solution(13734268297202334398)
XLA Ops:
  0.0 1.3 %dynamic-slice_bitcast_fusion.1 = (bf16[1,1024,128]{2,1,0:T(8,128)(2,1)S(1)}, bf16[1,1024,128]{2,1,0:T(8,128)(2,1)S(1)}, bf16[1,1024,128]{2,1,0:T(8,128)(2,1)S(1)}, bf16[1,1024,128]{2,1,0:T(8,128)(2,1)S(1)}) fusion(bf16[4096,128]{1,0:T(8,128)(2,1)} %param.2, s32[]{:T(128)S(6)} %select_n.156, s32[]{:T(128)S(6)} %select_n.155, s32[]{:T(128)S(6)} %select_n.154, ...), kind=kLoop, calls=%fused_computation.3 | loop fusion | bytes 2097168 | tf_op jit(solution)/shard_map/broadcast_in_dim | solution.py:173
  1.3 2.1 %collective-permute-start = (bf16[1,1024,128]{2,1,0:T(8,128)(2,1)S(1)}, bf16[1,1024,128]{2,1,0:T(8,128)(2,1)S(1)}, u32[]{:S(2)}, u32[]{:S(2)}) collective-permute-start(bf16[1,1024,128]{2,1,0:T(8,128)(2,1)S(1)} %get-tuple-element.26), channel_id=1, source_target_pairs={{0,4},{1,5},{2,6},{3,7},{4,0},{5,1},{6,2},{7,3},{8,12},{9,13},{10,... | collective-permute-start | bytes 786440 | tf_op jit(solution)/shard_map/ppermute | solution.py:210
  3.4 2.7 %collective-permute-start.2 = (bf16[1,1024,128]{2,1,0:T(8,128)(2,1)S(1)}, bf16[1,1024,128]{2,1,0:T(8,128)(2,1)S(1)}, u32[]{:S(2)}, u32[]{:S(2)}) collective-permute-start(bf16[1,1024,128]{2,1,0:T(8,128)(2,1)S(1)} %get-tuple-element.25), channel_id=1, source_target_pairs={{0,32},{1,33},{2,34},{3,35},{4,36},{5,37},{6,38},{7,39},{8,104},{9... | collective-permute-start | bytes 786440 | tf_op jit(solution)/shard_map/ppermute | solution.py:210
  6.1 0.0 collective-permute-start.3
  6.1 0.0 collective-permute-start.5
  6.1 2.5 %collective-permute-start.12 = (bf16[1,256,2048]{2,1,0:T(8,128)(2,1)}, bf16[1,256,2048]{2,1,0:T(8,128)(2,1)S(1)}, u32[]{:S(2)}, u32[]{:S(2)}) collective-permute-start(bf16[1,256,2048]{2,1,0:T(8,128)(2,1)} %bitcast.12.refs_4_), channel_id=1, source_target_pairs={{0,16},{1,17},{2,18},{3,19},{4,20},{5,21},{6,22},{7,23},{8,24},{9,... | collective-permute-start | bytes 3145736 | tf_op jit(solution)/shard_map/ppermute | solution.py:210
  8.6 0.3 collective-permute-done
  8.9 3.5 %collective-permute-start.1 = (bf16[1,1024,128]{2,1,0:T(8,128)(2,1)S(1)}, bf16[1,1024,128]{2,1,0:T(8,128)(2,1)S(1)}, u32[]{:S(2)}, u32[]{:S(2)}) collective-permute-start(bf16[1,1024,128]{2,1,0:T(8,128)(2,1)S(1)} %get-tuple-element.15), channel_id=1, source_target_pairs={{0,64},{1,65},{2,66},{3,67},{4,68},{5,69},{6,70},{7,71},{8,72},{9,... | collective-permute-start | bytes 786440 | tf_op jit(solution)/shard_map/ppermute | solution.py:210
  12.4 0.0 collective-permute-done.2
  12.4 1.9 %collective-permute-done.3 = bf16[1,1024,128]{2,1,0:T(8,128)(2,1)S(1)} collective-permute-done((bf16[1,1024,128]{2,1,0:T(8,128)(2,1)S(1)}, bf16[1,1024,128]{2,1,0:T(8,128)(2,1)S(1)}, u32[]{:S(2)}, u32[]{:S(2)}) %collective-permute-start.3) | collective-permute-done | bytes 262176 | tf_op jit(solution)/shard_map/ppermute | solution.py:210
  14.3 0.1 pad_maximum_fusion.refs_0_
  14.5 3.8 %collective-permute-start.15 = (bf16[4,1024,128]{2,1,0:T(8,128)(2,1)S(1)}, bf16[4,1024,128]{2,1,0:T(8,128)(2,1)S(1)}, u32[]{:S(2)}, u32[]{:S(2)}) collective-permute-start(bf16[4,1024,128]{2,1,0:T(8,128)(2,1)S(1)} %pad_maximum_fusion.refs_0_), channel_id=1, source_target_pairs={{0,1},{1,2},{2,3},{3,0},{4,5},{5,6},{6,7},{7,4},{8,11},{9,8},{10,9... | collective-permute-start | bytes 3145736 | tf_op jit(solution)/shard_map/ppermute | solution.py:210
  18.3 0.0 collective-permute-start.13
  18.3 13.2 %collective-permute-done.1 = bf16[1,1024,128]{2,1,0:T(8,128)(2,1)S(1)} collective-permute-done((bf16[1,1024,128]{2,1,0:T(8,128)(2,1)S(1)}, bf16[1,1024,128]{2,1,0:T(8,128)(2,1)S(1)}, u32[]{:S(2)}, u32[]{:S(2)}) %collective-permute-start.1) | collective-permute-done | bytes 262176 | tf_op jit(solution)/shard_map/ppermute | solution.py:210
  31.5 0.1 pad_maximum_fusion.1
  31.6 0.1 collective-permute-start.4
  31.7 0.0 collective-permute-done.5.refs_12_
  31.7 0.1 collective-permute-start.6
  31.8 1.8 %collective-permute-done.12.refs_5_ = bf16[1,256,2048]{2,1,0:T(8,128)(2,1)S(1)} collective-permute-done((bf16[1,256,2048]{2,1,0:T(8,128)(2,1)}, bf16[1,256,2048]{2,1,0:T(8,128)(2,1)S(1)}, u32[]{:S(2)}, u32[]{:S(2)}) %collective-permute-start.12) | collective-permute-done | bytes 1048608 | tf_op jit(solution)/shard_map/ppermute | solution.py:210
  33.5 3.2 %collective-permute-start.10 = (bf16[1,256,2048]{2,1,0:T(8,128)(2,1)}, bf16[1,256,2048]{2,1,0:T(8,128)(2,1)}, u32[]{:S(2)}, u32[]{:S(2)}) collective-permute-start(bf16[1,256,2048]{2,1,0:T(8,128)(2,1)} %bitcast.12.refs_4_), channel_id=1, source_target_pairs={{0,32},{1,33},{2,34},{3,35},{4,36},{5,37},{6,38},{7,39},{8,104},{9... | collective-permute-start | bytes 3145736 | tf_op jit(solution)/shard_map/ppermute | solution.py:210
  36.7 4.2 %collective-permute-done.15.refs_1_ = bf16[4,1024,128]{2,1,0:T(8,128)(2,1)S(1)} collective-permute-done((bf16[4,1024,128]{2,1,0:T(8,128)(2,1)S(1)}, bf16[4,1024,128]{2,1,0:T(8,128)(2,1)S(1)}, u32[]{:S(2)}, u32[]{:S(2)}) %collective-permute-start.15) | collective-permute-done | bytes 1048608 | tf_op jit(solution)/shard_map/ppermute | solution.py:210
  41.0 3.4 %collective-permute-start.16 = (bf16[4,1024,128]{2,1,0:T(8,128)(2,1)S(1)}, bf16[4,1024,128]{2,1,0:T(8,128)(2,1)S(1)}, u32[]{:S(2)}, u32[]{:S(2)}) collective-permute-start(bf16[4,1024,128]{2,1,0:T(8,128)(2,1)S(1)} %collective-permute-done.15.refs_1_), channel_id=1, source_target_pairs={{0,1},{1,2},{2,3},{3,0},{4,5},{5,6},{6,7},{7,4},{8,11},{9,8},{10,9... | collective-permute-start | bytes 3145736 | tf_op jit(solution)/shard_map/ppermute | solution.py:210
  44.4 0.0 collective-permute-done.13.refs_3_
  44.4 0.0 collective-permute-start.14
  44.4 5.3 %collective-permute-done.4 = bf16[3,1024,128]{2,1,0:T(8,128)(2,1)S(1)} collective-permute-done((bf16[3,1024,128]{2,1,0:T(8,128)(2,1)S(1)}, bf16[3,1024,128]{2,1,0:T(8,128)(2,1)S(1)}, u32[]{:S(2)}, u32[]{:S(2)}) %collective-permute-start.4) | collective-permute-done | bytes 786464 | tf_op jit(solution)/shard_map/ppermute | solution.py:210
  49.7 0.0 collective-permute-start.20
  49.7 0.7 constant_dynamic-update-slice_fusion.1
  50.4 1.0 constant_dynamic-update-slice_fusion.refs_4_.refs_0_
  51.4 0.0 collective-permute-done.6.refs_14_
  51.4 0.5 collective-permute-start.21
  51.9 0.0 collective-permute-done.10.refs_8_
  51.9 4.0 %collective-permute-start.7 = (bf16[4,1024,128]{2,1,0:T(8,128)(2,1)}, bf16[4,1024,128]{2,1,0:T(8,128)(2,1)}, u32[]{:S(2)}, u32[]{:S(2)}) collective-permute-start(bf16[4,1024,128]{2,1,0:T(8,128)(2,1)} %constant_dynamic-update-slice_fusion.refs_4_.refs_0_), channel_id=1, source_target_pairs={{0,1},{1,2},{2,3},{3,0},{4,5},{5,6},{6,7},{7,4},{8,11},{9,8},{10,9... | collective-permute-start | bytes 3145736 | tf_op jit(solution)/shard_map/ppermute | solution.py:210
  55.9 0.2 collective-permute-done.16.refs_2_
  56.1 0.0 copy-done
  56.1 2.5 %collective-permute-start.24 = (bf16[1,256,2048]{2,1,0:T(8,128)(2,1)}, bf16[1,256,2048]{2,1,0:T(8,128)(2,1)}, u32[]{:S(2)}, u32[]{:S(2)}) collective-permute-start(bf16[1,256,2048]{2,1,0:T(8,128)(2,1)} %collective-permute-done.5.refs_12_), channel_id=1, source_target_pairs={{0,16},{1,17},{2,18},{3,19},{4,20},{5,21},{6,22},{7,23},{8,24},{9,... | collective-permute-start | bytes 3145736 | tf_op jit(solution)/shard_map/ppermute | solution.py:210
  58.6 1.3 %collective-permute-done.14.refs_9_ = bf16[1,256,2048]{2,1,0:T(8,128)(2,1)} collective-permute-done((bf16[1,256,2048]{2,1,0:T(8,128)(2,1)S(1)}, bf16[1,256,2048]{2,1,0:T(8,128)(2,1)}, u32[]{:S(2)}, u32[]{:S(2)}) %collective-permute-start.14) | collective-permute-done | bytes 1048608 | tf_op jit(solution)/shard_map/ppermute | solution.py:210
  59.9 3.5 %collective-permute-start.11 = (bf16[1,256,2048]{2,1,0:T(8,128)(2,1)}, bf16[1,256,2048]{2,1,0:T(8,128)(2,1)}, u32[]{:S(2)}, u32[]{:S(2)}) collective-permute-start(bf16[1,256,2048]{2,1,0:T(8,128)(2,1)} %collective-permute-done.10.refs_8_), channel_id=1, source_target_pairs={{0,32},{1,33},{2,34},{3,35},{4,36},{5,37},{6,38},{7,39},{8,104},{9... | collective-permute-start | bytes 3145736 | tf_op jit(solution)/shard_map/ppermute | solution.py:210
  63.5 0.0 collective-permute-done.20.refs_6_
  63.5 0.1 collective-permute-start.17
  63.5 0.0 collective-permute-done.21.refs_7_
  63.5 0.9 copy-done.2
  64.4 1.6 %collective-permute-start.9 = (bf16[4,1024,128]{2,1,0:T(8,128)(2,1)}, bf16[4,1024,128]{2,1,0:T(8,128)(2,1)}, u32[]{:S(2)}, u32[]{:S(2)}) collective-permute-start(bf16[4,1024,128]{2,1,0:T(8,128)(2,1)} %constant_dynamic-update-slice_fusion.refs_4_.refs_0_), channel_id=1, source_target_pairs={{0,3},{1,0},{2,1},{3,2},{4,7},{5,4},{6,5},{7,6},{8,9},{9,10},{10,1... | collective-permute-start | bytes 3145736 | tf_op jit(solution)/shard_map/ppermute | solution.py:210
  66.1 1.9 %collective-permute-done.7.refs_5_.refs_1_ = bf16[4,1024,128]{2,1,0:T(8,128)(2,1)} collective-permute-done((bf16[4,1024,128]{2,1,0:T(8,128)(2,1)}, bf16[4,1024,128]{2,1,0:T(8,128)(2,1)}, u32[]{:S(2)}, u32[]{:S(2)}) %collective-permute-start.7) | collective-permute-done | bytes 1048608 | tf_op jit(solution)/shard_map/ppermute | solution.py:210
  67.9 3.4 %collective-permute-start.8 = (bf16[4,1024,128]{2,1,0:T(8,128)(2,1)}, bf16[4,1024,128]{2,1,0:T(8,128)(2,1)}, u32[]{:S(2)}, u32[]{:S(2)}) collective-permute-start(bf16[4,1024,128]{2,1,0:T(8,128)(2,1)} %collective-permute-done.7.refs_5_.refs_1_), channel_id=1, source_target_pairs={{0,1},{1,2},{2,3},{3,0},{4,5},{5,6},{6,7},{7,4},{8,11},{9,8},{10,9... | collective-permute-start | bytes 3145736 | tf_op jit(solution)/shard_map/ppermute | solution.py:210
  71.4 0.1 stack.95.place_ref
  71.4 9.5 %shard_map.28.refs_16_ = bf16[1024,2048]{1,0:T(8,128)(2,1)} custom-call(s32[8]{0:T(128)S(1)} %stack.95.place_ref, bf16[4,1024,128]{2,1,0:T(8,128)(2,1)S(1)} %pad_maximum_fusion.refs_0_, bf16[4,1024,128]{2,1,0:T(8,128)(2,1)S(1)} %collective-permute-done.15.refs_1_, bf16[4,1024,128]{2,1,0:T(8,128)(2,1)S(1)} %collective-permute-done.16.refs_2_, ...), custom_call_target="tpu_custom_call" | custom-call | flops 42949672 | bytes 209715 | tf_op jit(solution)/shard_map/pallas_call | solution.py:143
  80.9 0.5 collective-permute-done.24.refs_13_
  81.4 2.1 %collective-permute-start.25 = (bf16[1,256,2048]{2,1,0:T(8,128)(2,1)}, bf16[1,256,2048]{2,1,0:T(8,128)(2,1)}, u32[]{:S(2)}, u32[]{:S(2)}) collective-permute-start(bf16[1,256,2048]{2,1,0:T(8,128)(2,1)} %collective-permute-done.24.refs_13_), channel_id=1, source_target_pairs={{0,8},{1,9},{2,10},{3,11},{4,12},{5,13},{6,14},{7,15},{8,0},{9,1},... | collective-permute-start | bytes 3145736 | tf_op jit(solution)/shard_map/ppermute | solution.py:210
  83.5 0.0 collective-permute-done.11.refs_4_
  83.5 0.0 collective-permute-start.22
  83.5 3.2 %collective-permute-done.17.refs_5_ = bf16[1,256,2048]{2,1,0:T(8,128)(2,1)} collective-permute-done((bf16[1,256,2048]{2,1,0:T(8,128)(2,1)}, bf16[1,256,2048]{2,1,0:T(8,128)(2,1)}, u32[]{:S(2)}, u32[]{:S(2)}) %collective-permute-start.17) | collective-permute-done | bytes 1048608 | tf_op jit(solution)/shard_map/ppermute | solution.py:210
  86.7 4.9 %collective-permute-start.23 = (bf16[1,256,2048]{2,1,0:T(8,128)(2,1)}, bf16[1,256,2048]{2,1,0:T(8,128)(2,1)}, u32[]{:S(2)}, u32[]{:S(2)}) collective-permute-start(bf16[1,256,2048]{2,1,0:T(8,128)(2,1)} %collective-permute-done.14.refs_9_), channel_id=1, source_target_pairs={{0,8},{1,9},{2,10},{3,11},{4,12},{5,13},{6,14},{7,15},{8,0},{9,1},... | collective-permute-start | bytes 3145736 | tf_op jit(solution)/shard_map/ppermute | solution.py:210
  91.6 0.0 collective-permute-done.9.refs_7_.refs_3_
  91.6 1.0 collective-permute-start.18
  92.7 0.8 collective-permute-done.8.refs_6_.refs_2_
  93.5 0.0 collective-permute-start.19
  93.5 0.1 stack.112.place_ref
  93.6 0.0 collective-permute-done.25.refs_15_
  93.6 0.0 collective-permute-done.22.refs_10_
  93.6 0.6 collective-permute-done.23.refs_11_
  94.2 15.4 %shard_map.29.refs_8_ = bf16[1024,2048]{1,0:T(8,128)(2,1)} custom-call(s32[16]{0:T(128)S(1)} %stack.112.place_ref, bf16[4,1024,128]{2,1,0:T(8,128)(2,1)S(1)} %pad_maximum_fusion.refs_0_, bf16[4,1024,128]{2,1,0:T(8,128)(2,1)S(1)} %collective-permute-done.15.refs_1_, bf16[4,1024,128]{2,1,0:T(8,128)(2,1)S(1)} %collective-permute-done.16.refs_2_, ...), custom_call_target="tpu_custom_call" | custom-call | flops 8589934592 | bytes 20971520 | tf_op jit(solution)/shard_map/pallas_call | solution.py:143
  109.7 0.0 collective-permute-done.18.refs_6_
  109.7 0.0 collective-permute-done.19.refs_7_
  109.7 10.8 %shard_map.30 = bf16[1024,2048]{1,0:T(8,128)(2,1)} custom-call(s32[8]{0:T(128)S(1)} %stack.95.place_ref, bf16[4,1024,128]{2,1,0:T(8,128)(2,1)} %constant_dynamic-update-slice_fusion.refs_4_.refs_0_, bf16[4,1024,128]{2,1,0:T(8,128)(2,1)} %collective-permute-done.7.refs_5_.refs_1_, bf16[4,1024,128]{2,1,0:T(8,128)(2,1)} %collective-permute-done.8.refs_6_.refs_2_, ...), custom_call_target="tpu_custom_call" | custom-call | flops 12884901888 | bytes 62914560 | tf_op jit(solution)/shard_map/pallas_call | solution.py:143
  (8 shorter events, 0.0 us)
Async XLA Ops:
  1.3 7.6 %collective-permute-start = (bf16[1,1024,128]{2,1,0:T(8,128)(2,1)S(1)}, bf16[1,1024,128]{2,1,0:T(8,128)(2,1)S(1)}, u32[]{:S(2)}, u32[]{:S(2)}) collective-permute-start(bf16[1,1024,128]{2,1,0:T(8,128)(2,1)S(1)} %get-tuple-element.26), channel_id=1, source_target_pairs={{0,4},{1,5},{2,6},{3,7},{4,0},{5,1},{6,2},{7,3},{8,12},{9,13},{10,... | collective-permute-start | bytes 786440 | tf_op jit(solution)/shard_map/ppermute | solution.py:210
  3.4 9.1 %collective-permute-start.2 = (bf16[1,1024,128]{2,1,0:T(8,128)(2,1)S(1)}, bf16[1,1024,128]{2,1,0:T(8,128)(2,1)S(1)}, u32[]{:S(2)}, u32[]{:S(2)}) collective-permute-start(bf16[1,1024,128]{2,1,0:T(8,128)(2,1)S(1)} %get-tuple-element.25), channel_id=1, source_target_pairs={{0,32},{1,33},{2,34},{3,35},{4,36},{5,37},{6,38},{7,39},{8,104},{9... | collective-permute-start | bytes 786440 | tf_op jit(solution)/shard_map/ppermute | solution.py:210
  6.1 8.2 %collective-permute-start.3 = (bf16[1,1024,128]{2,1,0:T(8,128)(2,1)S(1)}, bf16[1,1024,128]{2,1,0:T(8,128)(2,1)S(1)}, u32[]{:S(2)}, u32[]{:S(2)}) collective-permute-start(bf16[1,1024,128]{2,1,0:T(8,128)(2,1)S(1)} %get-tuple-element.28), channel_id=1, source_target_pairs={{0,96},{1,97},{2,98},{3,99},{4,100},{5,101},{6,102},{7,103},{8,40}... | collective-permute-start | bytes 786440 | tf_op jit(solution)/shard_map/ppermute | solution.py:210
  6.1 25.5 %collective-permute-start.5 = (bf16[1,256,2048]{2,1,0:T(8,128)(2,1)}, bf16[1,256,2048]{2,1,0:T(8,128)(2,1)}, u32[]{:S(2)}, u32[]{:S(2)}) collective-permute-start(bf16[1,256,2048]{2,1,0:T(8,128)(2,1)} %bitcast.12.refs_4_), channel_id=1, source_target_pairs={{0,96},{1,97},{2,98},{3,99},{4,100},{5,101},{6,102},{7,103},{8,40}... | collective-permute-start | bytes 3145736 | tf_op jit(solution)/shard_map/ppermute | solution.py:210
  6.1 27.4 %collective-permute-start.12 = (bf16[1,256,2048]{2,1,0:T(8,128)(2,1)}, bf16[1,256,2048]{2,1,0:T(8,128)(2,1)S(1)}, u32[]{:S(2)}, u32[]{:S(2)}) collective-permute-start(bf16[1,256,2048]{2,1,0:T(8,128)(2,1)} %bitcast.12.refs_4_), channel_id=1, source_target_pairs={{0,16},{1,17},{2,18},{3,19},{4,20},{5,21},{6,22},{7,23},{8,24},{9,... | collective-permute-start | bytes 3145736 | tf_op jit(solution)/shard_map/ppermute | solution.py:210
  8.9 22.6 %collective-permute-start.1 = (bf16[1,1024,128]{2,1,0:T(8,128)(2,1)S(1)}, bf16[1,1024,128]{2,1,0:T(8,128)(2,1)S(1)}, u32[]{:S(2)}, u32[]{:S(2)}) collective-permute-start(bf16[1,1024,128]{2,1,0:T(8,128)(2,1)S(1)} %get-tuple-element.15), channel_id=1, source_target_pairs={{0,64},{1,65},{2,66},{3,67},{4,68},{5,69},{6,70},{7,71},{8,72},{9,... | collective-permute-start | bytes 786440 | tf_op jit(solution)/shard_map/ppermute | solution.py:210
  14.5 26.5 %collective-permute-start.15 = (bf16[4,1024,128]{2,1,0:T(8,128)(2,1)S(1)}, bf16[4,1024,128]{2,1,0:T(8,128)(2,1)S(1)}, u32[]{:S(2)}, u32[]{:S(2)}) collective-permute-start(bf16[4,1024,128]{2,1,0:T(8,128)(2,1)S(1)} %pad_maximum_fusion.refs_0_), channel_id=1, source_target_pairs={{0,1},{1,2},{2,3},{3,0},{4,5},{5,6},{6,7},{7,4},{8,11},{9,8},{10,9... | collective-permute-start | bytes 3145736 | tf_op jit(solution)/shard_map/ppermute | solution.py:210
  18.3 26.1 %collective-permute-start.13 = (bf16[4,1024,128]{2,1,0:T(8,128)(2,1)S(1)}, bf16[4,1024,128]{2,1,0:T(8,128)(2,1)S(1)}, u32[]{:S(2)}, u32[]{:S(2)}) collective-permute-start(bf16[4,1024,128]{2,1,0:T(8,128)(2,1)S(1)} %pad_maximum_fusion.refs_0_), channel_id=1, source_target_pairs={{0,3},{1,0},{2,1},{3,2},{4,7},{5,4},{6,5},{7,6},{8,9},{9,10},{10,1... | collective-permute-start | bytes 3145736 | tf_op jit(solution)/shard_map/ppermute | solution.py:210
  31.6 18.1 %collective-permute-start.4 = (bf16[3,1024,128]{2,1,0:T(8,128)(2,1)S(1)}, bf16[3,1024,128]{2,1,0:T(8,128)(2,1)S(1)}, u32[]{:S(2)}, u32[]{:S(2)}) collective-permute-start(bf16[3,1024,128]{2,1,0:T(8,128)(2,1)S(1)} %pad_maximum_fusion.1), channel_id=1, source_target_pairs={{0,4},{1,5},{2,6},{3,7},{4,0},{5,1},{6,2},{7,3},{8,12},{9,13},{10,... | collective-permute-start | bytes 2359304 | tf_op jit(solution)/shard_map/ppermute | solution.py:210
  31.7 19.7 %collective-permute-start.6 = (bf16[1,256,2048]{2,1,0:T(8,128)(2,1)}, bf16[1,256,2048]{2,1,0:T(8,128)(2,1)S(1)}, u32[]{:S(2)}, u32[]{:S(2)}) collective-permute-start(bf16[1,256,2048]{2,1,0:T(8,128)(2,1)} %collective-permute-done.5.refs_12_), channel_id=1, source_target_pairs={{0,8},{1,9},{2,10},{3,11},{4,12},{5,13},{6,14},{7,15},{8,0},{9,1},... | collective-permute-start | bytes 3145736 | tf_op jit(solution)/shard_map/ppermute | solution.py:210
  33.5 25.1 %copy-start.1 = (bf16[1,256,2048]{2,1,0:T(8,128)(2,1)}, bf16[1,256,2048]{2,1,0:T(8,128)(2,1)S(1)}, u32[]{:S(2)}) copy-start(bf16[1,256,2048]{2,1,0:T(8,128)(2,1)S(1)} %collective-permute-done.12.refs_5_) | copy-start | bytes 3145732
  33.5 18.4 %collective-permute-start.10 = (bf16[1,256,2048]{2,1,0:T(8,128)(2,1)}, bf16[1,256,2048]{2,1,0:T(8,128)(2,1)}, u32[]{:S(2)}, u32[]{:S(2)}) collective-permute-start(bf16[1,256,2048]{2,1,0:T(8,128)(2,1)} %bitcast.12.refs_4_), channel_id=1, source_target_pairs={{0,32},{1,33},{2,34},{3,35},{4,36},{5,37},{6,38},{7,39},{8,104},{9... | collective-permute-start | bytes 3145736 | tf_op jit(solution)/shard_map/ppermute | solution.py:210
  41.0 15.2 %collective-permute-start.16 = (bf16[4,1024,128]{2,1,0:T(8,128)(2,1)S(1)}, bf16[4,1024,128]{2,1,0:T(8,128)(2,1)S(1)}, u32[]{:S(2)}, u32[]{:S(2)}) collective-permute-start(bf16[4,1024,128]{2,1,0:T(8,128)(2,1)S(1)} %collective-permute-done.15.refs_1_), channel_id=1, source_target_pairs={{0,1},{1,2},{2,3},{3,0},{4,5},{5,6},{6,7},{7,4},{8,11},{9,8},{10,9... | collective-permute-start | bytes 3145736 | tf_op jit(solution)/shard_map/ppermute | solution.py:210
  44.4 11.7 %copy-start = (bf16[4,1024,128]{2,1,0:T(8,128)(2,1)}, bf16[4,1024,128]{2,1,0:T(8,128)(2,1)S(1)}, u32[]{:S(2)}) copy-start(bf16[4,1024,128]{2,1,0:T(8,128)(2,1)S(1)} %collective-permute-done.13.refs_3_) | copy-start | bytes 3145732
  44.4 15.6 %collective-permute-start.14 = (bf16[1,256,2048]{2,1,0:T(8,128)(2,1)S(1)}, bf16[1,256,2048]{2,1,0:T(8,128)(2,1)}, u32[]{:S(2)}, u32[]{:S(2)}) collective-permute-start(bf16[1,256,2048]{2,1,0:T(8,128)(2,1)S(1)} %collective-permute-done.12.refs_5_), channel_id=1, source_target_pairs={{0,32},{1,33},{2,34},{3,35},{4,36},{5,37},{6,38},{7,39},{8,104},{9... | collective-permute-start | bytes 3145736 | tf_op jit(solution)/shard_map/ppermute | solution.py:210
  49.7 13.8 %collective-permute-start.20 = (bf16[1,256,2048]{2,1,0:T(8,128)(2,1)}, bf16[1,256,2048]{2,1,0:T(8,128)(2,1)S(1)}, u32[]{:S(2)}, u32[]{:S(2)}) collective-permute-start(bf16[1,256,2048]{2,1,0:T(8,128)(2,1)} %bitcast.12.refs_4_), channel_id=1, source_target_pairs={{0,8},{1,9},{2,10},{3,11},{4,12},{5,13},{6,14},{7,15},{8,0},{9,1},... | collective-permute-start | bytes 3145736 | tf_op jit(solution)/shard_map/ppermute | solution.py:210
  51.4 16.6 %copy-start.4 = (bf16[1,256,2048]{2,1,0:T(8,128)(2,1)}, bf16[1,256,2048]{2,1,0:T(8,128)(2,1)S(1)}, u32[]{:S(2)}) copy-start(bf16[1,256,2048]{2,1,0:T(8,128)(2,1)S(1)} %collective-permute-done.6.refs_14_) | copy-start | bytes 3145732
  51.4 12.2 %collective-permute-start.21 = (bf16[1,256,2048]{2,1,0:T(8,128)(2,1)S(1)}, bf16[1,256,2048]{2,1,0:T(8,128)(2,1)S(1)}, u32[]{:S(2)}, u32[]{:S(2)}) collective-permute-start(bf16[1,256,2048]{2,1,0:T(8,128)(2,1)S(1)} %collective-permute-done.12.refs_5_), channel_id=1, source_target_pairs={{0,8},{1,9},{2,10},{3,11},{4,12},{5,13},{6,14},{7,15},{8,0},{9,1},... | collective-permute-start | bytes 3145736 | tf_op jit(solution)/shard_map/ppermute | solution.py:210
  51.9 16.1 %collective-permute-start.7 = (bf16[4,1024,128]{2,1,0:T(8,128)(2,1)}, bf16[4,1024,128]{2,1,0:T(8,128)(2,1)}, u32[]{:S(2)}, u32[]{:S(2)}) collective-permute-start(bf16[4,1024,128]{2,1,0:T(8,128)(2,1)} %constant_dynamic-update-slice_fusion.refs_4_.refs_0_), channel_id=1, source_target_pairs={{0,1},{1,2},{2,3},{3,0},{4,5},{5,6},{6,7},{7,4},{8,11},{9,8},{10,9... | collective-permute-start | bytes 3145736 | tf_op jit(solution)/shard_map/ppermute | solution.py:210
  56.1 25.3 %collective-permute-start.24 = (bf16[1,256,2048]{2,1,0:T(8,128)(2,1)}, bf16[1,256,2048]{2,1,0:T(8,128)(2,1)}, u32[]{:S(2)}, u32[]{:S(2)}) collective-permute-start(bf16[1,256,2048]{2,1,0:T(8,128)(2,1)} %collective-permute-done.5.refs_12_), channel_id=1, source_target_pairs={{0,16},{1,17},{2,18},{3,19},{4,20},{5,21},{6,22},{7,23},{8,24},{9,... | collective-permute-start | bytes 3145736 | tf_op jit(solution)/shard_map/ppermute | solution.py:210
  59.9 23.6 %collective-permute-start.11 = (bf16[1,256,2048]{2,1,0:T(8,128)(2,1)}, bf16[1,256,2048]{2,1,0:T(8,128)(2,1)}, u32[]{:S(2)}, u32[]{:S(2)}) collective-permute-start(bf16[1,256,2048]{2,1,0:T(8,128)(2,1)} %collective-permute-done.10.refs_8_), channel_id=1, source_target_pairs={{0,32},{1,33},{2,34},{3,35},{4,36},{5,37},{6,38},{7,39},{8,104},{9... | collective-permute-start | bytes 3145736 | tf_op jit(solution)/shard_map/ppermute | solution.py:210
  63.5 1.0 copy-start.2
  63.5 23.3 %collective-permute-start.17 = (bf16[1,256,2048]{2,1,0:T(8,128)(2,1)}, bf16[1,256,2048]{2,1,0:T(8,128)(2,1)}, u32[]{:S(2)}, u32[]{:S(2)}) collective-permute-start(bf16[1,256,2048]{2,1,0:T(8,128)(2,1)} %collective-permute-done.14.refs_9_), channel_id=1, source_target_pairs={{0,32},{1,33},{2,34},{3,35},{4,36},{5,37},{6,38},{7,39},{8,104},{9... | collective-permute-start | bytes 3145736 | tf_op jit(solution)/shard_map/ppermute | solution.py:210
  64.4 1.6 %copy-start.3 = (bf16[1,256,2048]{2,1,0:T(8,128)(2,1)}, bf16[1,256,2048]{2,1,0:T(8,128)(2,1)S(1)}, u32[]{:S(2)}) copy-start(bf16[1,256,2048]{2,1,0:T(8,128)(2,1)S(1)} %collective-permute-done.21.refs_7_) | copy-start | bytes 3145732
  64.4 27.2 %collective-permute-start.9 = (bf16[4,1024,128]{2,1,0:T(8,128)(2,1)}, bf16[4,1024,128]{2,1,0:T(8,128)(2,1)}, u32[]{:S(2)}, u32[]{:S(2)}) collective-permute-start(bf16[4,1024,128]{2,1,0:T(8,128)(2,1)} %constant_dynamic-update-slice_fusion.refs_4_.refs_0_), channel_id=1, source_target_pairs={{0,3},{1,0},{2,1},{3,2},{4,7},{5,4},{6,5},{7,6},{8,9},{9,10},{10,1... | collective-permute-start | bytes 3145736 | tf_op jit(solution)/shard_map/ppermute | solution.py:210
  67.9 25.5 %collective-permute-start.8 = (bf16[4,1024,128]{2,1,0:T(8,128)(2,1)}, bf16[4,1024,128]{2,1,0:T(8,128)(2,1)}, u32[]{:S(2)}, u32[]{:S(2)}) collective-permute-start(bf16[4,1024,128]{2,1,0:T(8,128)(2,1)} %collective-permute-done.7.refs_5_.refs_1_), channel_id=1, source_target_pairs={{0,1},{1,2},{2,3},{3,0},{4,5},{5,6},{6,7},{7,4},{8,11},{9,8},{10,9... | collective-permute-start | bytes 3145736 | tf_op jit(solution)/shard_map/ppermute | solution.py:210
  81.4 12.2 %collective-permute-start.25 = (bf16[1,256,2048]{2,1,0:T(8,128)(2,1)}, bf16[1,256,2048]{2,1,0:T(8,128)(2,1)}, u32[]{:S(2)}, u32[]{:S(2)}) collective-permute-start(bf16[1,256,2048]{2,1,0:T(8,128)(2,1)} %collective-permute-done.24.refs_13_), channel_id=1, source_target_pairs={{0,8},{1,9},{2,10},{3,11},{4,12},{5,13},{6,14},{7,15},{8,0},{9,1},... | collective-permute-start | bytes 3145736 | tf_op jit(solution)/shard_map/ppermute | solution.py:210
  83.5 10.1 %collective-permute-start.22 = (bf16[1,256,2048]{2,1,0:T(8,128)(2,1)}, bf16[1,256,2048]{2,1,0:T(8,128)(2,1)}, u32[]{:S(2)}, u32[]{:S(2)}) collective-permute-start(bf16[1,256,2048]{2,1,0:T(8,128)(2,1)} %collective-permute-done.10.refs_8_), channel_id=1, source_target_pairs={{0,8},{1,9},{2,10},{3,11},{4,12},{5,13},{6,14},{7,15},{8,0},{9,1},... | collective-permute-start | bytes 3145736 | tf_op jit(solution)/shard_map/ppermute | solution.py:210
  86.7 7.5 %collective-permute-start.23 = (bf16[1,256,2048]{2,1,0:T(8,128)(2,1)}, bf16[1,256,2048]{2,1,0:T(8,128)(2,1)}, u32[]{:S(2)}, u32[]{:S(2)}) collective-permute-start(bf16[1,256,2048]{2,1,0:T(8,128)(2,1)} %collective-permute-done.14.refs_9_), channel_id=1, source_target_pairs={{0,8},{1,9},{2,10},{3,11},{4,12},{5,13},{6,14},{7,15},{8,0},{9,1},... | collective-permute-start | bytes 3145736 | tf_op jit(solution)/shard_map/ppermute | solution.py:210
  91.6 18.1 %collective-permute-start.18 = (bf16[1,256,2048]{2,1,0:T(8,128)(2,1)}, bf16[1,256,2048]{2,1,0:T(8,128)(2,1)}, u32[]{:S(2)}, u32[]{:S(2)}) collective-permute-start(bf16[1,256,2048]{2,1,0:T(8,128)(2,1)} %collective-permute-done.11.refs_4_), channel_id=1, source_target_pairs={{0,8},{1,9},{2,10},{3,11},{4,12},{5,13},{6,14},{7,15},{8,0},{9,1},... | collective-permute-start | bytes 3145736 | tf_op jit(solution)/shard_map/ppermute | solution.py:210
  93.5 16.2 %collective-permute-start.19 = (bf16[1,256,2048]{2,1,0:T(8,128)(2,1)}, bf16[1,256,2048]{2,1,0:T(8,128)(2,1)}, u32[]{:S(2)}, u32[]{:S(2)}) collective-permute-start(bf16[1,256,2048]{2,1,0:T(8,128)(2,1)} %collective-permute-done.17.refs_5_), channel_id=1, source_target_pairs={{0,8},{1,9},{2,10},{3,11},{4,12},{5,13},{6,14},{7,15},{8,0},{9,1},... | collective-permute-start | bytes 3145736 | tf_op jit(solution)/shard_map/ppermute | solution.py:210

commit v4 on v3

--- a/solution.py
+++ b/solution.py
@@ -107,8 +107,8 @@
     @pl.when(first)
     def _():
         for top in range(0, 1024, SPAN):
-            for copy in copies(top):
-                copy.start()
+            for i, copy in enumerate(copies(top)):
+                copy.start(priority=i % 2)
 
     rhs = jnp.concatenate([ref[...].reshape(-1, tile) for ref in b_refs], axis=0)
     for top in range(0, 1024, SPAN):

time: 121 us -> 121 us (level)
  transfers between devices with their start and end apart: 26 -> 26, of which waited for: 13 -> 13; matrix products, arithmetic and copies ran while one was open for 2% -> 2% of each run, Pallas kernels for 21% -> 20%
where the time goes in v4:
time: 121 us; the launch traced here: 120 us
  starting transfers between devices  45.2 us (37%)
  Pallas kernels  35.4 us (29%)
  waiting for transfers between devices  35.3 us (29%)
  local copies, waits for them, and re-layouts  4.01 us (3%)
    ppermute x26, starting transfers between devices, local(): held[name] = lax.ppermute(sent, AXES, how)  45.2 us
    pallas_call x3, Pallas kernels, multiply(): pl.pallas_call(functools.partial(kernel, tile, tuple(places), n_a, n_b, h...  35.4 us
    ppermute x26, waiting for transfers between devices, local(): held[name] = lax.ppermute(sent, AXES, how)  35.3 us
  transfers between devices with their start and end apart: 26, of which 13 were waited for; matrix products, arithmetic and copies ran while one was open for 2% of the time, Pallas kernels for 20%

profile of v4, /device:TPU:1, one launch (start us, length us, event | category | flops | bytes accessed | tf_op | source)
XLA Modules:
  0.0 120.4 jit_solution(13793680817151468704)
XLA Ops:
  0.0 1.3 %dynamic-slice_bitcast_fusion.1 = (bf16[1,1024,128]{2,1,0:T(8,128)(2,1)S(1)}, bf16[1,1024,128]{2,1,0:T(8,128)(2,1)S(1)}, bf16[1,1024,128]{2,1,0:T(8,128)(2,1)S(1)}, bf16[1,1024,128]{2,1,0:T(8,128)(2,1)S(1)}) fusion(bf16[4096,128]{1,0:T(8,128)(2,1)} %param.2, s32[]{:T(128)S(6)} %select_n.156, s32[]{:T(128)S(6)} %select_n.155, s32[]{:T(128)S(6)} %select_n.154, ...), kind=kLoop, calls=%fused_computation.3 | loop fusion | bytes 2097168 | tf_op jit(solution)/shard_map/broadcast_in_dim | solution.py:173
  1.3 2.1 %collective-permute-start = (bf16[1,1024,128]{2,1,0:T(8,128)(2,1)S(1)}, bf16[1,1024,128]{2,1,0:T(8,128)(2,1)S(1)}, u32[]{:S(2)}, u32[]{:S(2)}) collective-permute-start(bf16[1,1024,128]{2,1,0:T(8,128)(2,1)S(1)} %get-tuple-element.26), channel_id=1, source_target_pairs={{0,4},{1,5},{2,6},{3,7},{4,0},{5,1},{6,2},{7,3},{8,12},{9,13},{10,... | collective-permute-start | bytes 786440 | tf_op jit(solution)/shard_map/ppermute | solution.py:210
  3.4 2.7 %collective-permute-start.2 = (bf16[1,1024,128]{2,1,0:T(8,128)(2,1)S(1)}, bf16[1,1024,128]{2,1,0:T(8,128)(2,1)S(1)}, u32[]{:S(2)}, u32[]{:S(2)}) collective-permute-start(bf16[1,1024,128]{2,1,0:T(8,128)(2,1)S(1)} %get-tuple-element.25), channel_id=1, source_target_pairs={{0,32},{1,33},{2,34},{3,35},{4,36},{5,37},{6,38},{7,39},{8,104},{9... | collective-permute-start | bytes 786440 | tf_op jit(solution)/shard_map/ppermute | solution.py:210
  6.1 0.0 collective-permute-start.3
  6.1 0.0 collective-permute-start.5
  6.1 2.5 %collective-permute-start.12 = (bf16[1,256,2048]{2,1,0:T(8,128)(2,1)}, bf16[1,256,2048]{2,1,0:T(8,128)(2,1)S(1)}, u32[]{:S(2)}, u32[]{:S(2)}) collective-permute-start(bf16[1,256,2048]{2,1,0:T(8,128)(2,1)} %bitcast.12.refs_4_), channel_id=1, source_target_pairs={{0,16},{1,17},{2,18},{3,19},{4,20},{5,21},{6,22},{7,23},{8,24},{9,... | collective-permute-start | bytes 3145736 | tf_op jit(solution)/shard_map/ppermute | solution.py:210
  8.6 0.3 collective-permute-done
  8.9 3.5 %collective-permute-start.1 = (bf16[1,1024,128]{2,1,0:T(8,128)(2,1)S(1)}, bf16[1,1024,128]{2,1,0:T(8,128)(2,1)S(1)}, u32[]{:S(2)}, u32[]{:S(2)}) collective-permute-start(bf16[1,1024,128]{2,1,0:T(8,128)(2,1)S(1)} %get-tuple-element.15), channel_id=1, source_target_pairs={{0,64},{1,65},{2,66},{3,67},{4,68},{5,69},{6,70},{7,71},{8,72},{9,... | collective-permute-start | bytes 786440 | tf_op jit(solution)/shard_map/ppermute | solution.py:210
  12.4 0.0 collective-permute-done.2
  12.4 1.9 %collective-permute-done.3 = bf16[1,1024,128]{2,1,0:T(8,128)(2,1)S(1)} collective-permute-done((bf16[1,1024,128]{2,1,0:T(8,128)(2,1)S(1)}, bf16[1,1024,128]{2,1,0:T(8,128)(2,1)S(1)}, u32[]{:S(2)}, u32[]{:S(2)}) %collective-permute-start.3) | collective-permute-done | bytes 262176 | tf_op jit(solution)/shard_map/ppermute | solution.py:210
  14.3 0.1 pad_maximum_fusion.refs_0_
  14.5 3.8 %collective-permute-start.15 = (bf16[4,1024,128]{2,1,0:T(8,128)(2,1)S(1)}, bf16[4,1024,128]{2,1,0:T(8,128)(2,1)S(1)}, u32[]{:S(2)}, u32[]{:S(2)}) collective-permute-start(bf16[4,1024,128]{2,1,0:T(8,128)(2,1)S(1)} %pad_maximum_fusion.refs_0_), channel_id=1, source_target_pairs={{0,1},{1,2},{2,3},{3,0},{4,5},{5,6},{6,7},{7,4},{8,11},{9,8},{10,9... | collective-permute-start | bytes 3145736 | tf_op jit(solution)/shard_map/ppermute | solution.py:210
  18.3 0.0 collective-permute-start.13
  18.3 13.2 %collective-permute-done.1 = bf16[1,1024,128]{2,1,0:T(8,128)(2,1)S(1)} collective-permute-done((bf16[1,1024,128]{2,1,0:T(8,128)(2,1)S(1)}, bf16[1,1024,128]{2,1,0:T(8,128)(2,1)S(1)}, u32[]{:S(2)}, u32[]{:S(2)}) %collective-permute-start.1) | collective-permute-done | bytes 262176 | tf_op jit(solution)/shard_map/ppermute | solution.py:210
  31.5 0.1 pad_maximum_fusion.1
  31.6 0.1 collective-permute-start.4
  31.7 0.0 collective-permute-done.5.refs_12_
  31.7 0.1 collective-permute-start.6
  31.8 1.8 %collective-permute-done.12.refs_5_ = bf16[1,256,2048]{2,1,0:T(8,128)(2,1)S(1)} collective-permute-done((bf16[1,256,2048]{2,1,0:T(8,128)(2,1)}, bf16[1,256,2048]{2,1,0:T(8,128)(2,1)S(1)}, u32[]{:S(2)}, u32[]{:S(2)}) %collective-permute-start.12) | collective-permute-done | bytes 1048608 | tf_op jit(solution)/shard_map/ppermute | solution.py:210
  33.5 3.2 %collective-permute-start.10 = (bf16[1,256,2048]{2,1,0:T(8,128)(2,1)}, bf16[1,256,2048]{2,1,0:T(8,128)(2,1)}, u32[]{:S(2)}, u32[]{:S(2)}) collective-permute-start(bf16[1,256,2048]{2,1,0:T(8,128)(2,1)} %bitcast.12.refs_4_), channel_id=1, source_target_pairs={{0,32},{1,33},{2,34},{3,35},{4,36},{5,37},{6,38},{7,39},{8,104},{9... | collective-permute-start | bytes 3145736 | tf_op jit(solution)/shard_map/ppermute | solution.py:210
  36.7 4.2 %collective-permute-done.15.refs_1_ = bf16[4,1024,128]{2,1,0:T(8,128)(2,1)S(1)} collective-permute-done((bf16[4,1024,128]{2,1,0:T(8,128)(2,1)S(1)}, bf16[4,1024,128]{2,1,0:T(8,128)(2,1)S(1)}, u32[]{:S(2)}, u32[]{:S(2)}) %collective-permute-start.15) | collective-permute-done | bytes 1048608 | tf_op jit(solution)/shard_map/ppermute | solution.py:210
  41.0 3.4 %collective-permute-start.16 = (bf16[4,1024,128]{2,1,0:T(8,128)(2,1)S(1)}, bf16[4,1024,128]{2,1,0:T(8,128)(2,1)S(1)}, u32[]{:S(2)}, u32[]{:S(2)}) collective-permute-start(bf16[4,1024,128]{2,1,0:T(8,128)(2,1)S(1)} %collective-permute-done.15.refs_1_), channel_id=1, source_target_pairs={{0,1},{1,2},{2,3},{3,0},{4,5},{5,6},{6,7},{7,4},{8,11},{9,8},{10,9... | collective-permute-start | bytes 3145736 | tf_op jit(solution)/shard_map/ppermute | solution.py:210
  44.4 0.0 collective-permute-done.13.refs_3_
  44.4 0.0 collective-permute-start.14
  44.4 5.3 %collective-permute-done.4 = bf16[3,1024,128]{2,1,0:T(8,128)(2,1)S(1)} collective-permute-done((bf16[3,1024,128]{2,1,0:T(8,128)(2,1)S(1)}, bf16[3,1024,128]{2,1,0:T(8,128)(2,1)S(1)}, u32[]{:S(2)}, u32[]{:S(2)}) %collective-permute-start.4) | collective-permute-done | bytes 786464 | tf_op jit(solution)/shard_map/ppermute | solution.py:210
  49.7 0.0 collective-permute-start.20
  49.7 0.7 constant_dynamic-update-slice_fusion.1
  50.4 1.0 constant_dynamic-update-slice_fusion.refs_4_.refs_0_
  51.4 0.0 collective-permute-done.6.refs_14_
  51.4 0.5 collective-permute-start.21
  51.9 0.0 collective-permute-done.10.refs_8_
  51.9 4.0 %collective-permute-start.7 = (bf16[4,1024,128]{2,1,0:T(8,128)(2,1)}, bf16[4,1024,128]{2,1,0:T(8,128)(2,1)}, u32[]{:S(2)}, u32[]{:S(2)}) collective-permute-start(bf16[4,1024,128]{2,1,0:T(8,128)(2,1)} %constant_dynamic-update-slice_fusion.refs_4_.refs_0_), channel_id=1, source_target_pairs={{0,1},{1,2},{2,3},{3,0},{4,5},{5,6},{6,7},{7,4},{8,11},{9,8},{10,9... | collective-permute-start | bytes 3145736 | tf_op jit(solution)/shard_map/ppermute | solution.py:210
  55.9 0.2 collective-permute-done.16.refs_2_
  56.1 0.0 copy-done
  56.1 2.5 %collective-permute-start.24 = (bf16[1,256,2048]{2,1,0:T(8,128)(2,1)}, bf16[1,256,2048]{2,1,0:T(8,128)(2,1)}, u32[]{:S(2)}, u32[]{:S(2)}) collective-permute-start(bf16[1,256,2048]{2,1,0:T(8,128)(2,1)} %collective-permute-done.5.refs_12_), channel_id=1, source_target_pairs={{0,16},{1,17},{2,18},{3,19},{4,20},{5,21},{6,22},{7,23},{8,24},{9,... | collective-permute-start | bytes 3145736 | tf_op jit(solution)/shard_map/ppermute | solution.py:210
  58.6 1.3 %collective-permute-done.14.refs_9_ = bf16[1,256,2048]{2,1,0:T(8,128)(2,1)} collective-permute-done((bf16[1,256,2048]{2,1,0:T(8,128)(2,1)S(1)}, bf16[1,256,2048]{2,1,0:T(8,128)(2,1)}, u32[]{:S(2)}, u32[]{:S(2)}) %collective-permute-start.14) | collective-permute-done | bytes 1048608 | tf_op jit(solution)/shard_map/ppermute | solution.py:210
  59.9 3.5 %collective-permute-start.11 = (bf16[1,256,2048]{2,1,0:T(8,128)(2,1)}, bf16[1,256,2048]{2,1,0:T(8,128)(2,1)}, u32[]{:S(2)}, u32[]{:S(2)}) collective-permute-start(bf16[1,256,2048]{2,1,0:T(8,128)(2,1)} %collective-permute-done.10.refs_8_), channel_id=1, source_target_pairs={{0,32},{1,33},{2,34},{3,35},{4,36},{5,37},{6,38},{7,39},{8,104},{9... | collective-permute-start | bytes 3145736 | tf_op jit(solution)/shard_map/ppermute | solution.py:210
  63.5 0.0 collective-permute-done.20.refs_6_
  63.5 0.1 collective-permute-start.17
  63.5 0.0 collective-permute-done.21.refs_7_
  63.5 0.9 copy-done.2
  64.4 1.6 %collective-permute-start.9 = (bf16[4,1024,128]{2,1,0:T(8,128)(2,1)}, bf16[4,1024,128]{2,1,0:T(8,128)(2,1)}, u32[]{:S(2)}, u32[]{:S(2)}) collective-permute-start(bf16[4,1024,128]{2,1,0:T(8,128)(2,1)} %constant_dynamic-update-slice_fusion.refs_4_.refs_0_), channel_id=1, source_target_pairs={{0,3},{1,0},{2,1},{3,2},{4,7},{5,4},{6,5},{7,6},{8,9},{9,10},{10,1... | collective-permute-start | bytes 3145736 | tf_op jit(solution)/shard_map/ppermute | solution.py:210
  66.1 1.9 %collective-permute-done.7.refs_5_.refs_1_ = bf16[4,1024,128]{2,1,0:T(8,128)(2,1)} collective-permute-done((bf16[4,1024,128]{2,1,0:T(8,128)(2,1)}, bf16[4,1024,128]{2,1,0:T(8,128)(2,1)}, u32[]{:S(2)}, u32[]{:S(2)}) %collective-permute-start.7) | collective-permute-done | bytes 1048608 | tf_op jit(solution)/shard_map/ppermute | solution.py:210
  67.9 3.4 %collective-permute-start.8 = (bf16[4,1024,128]{2,1,0:T(8,128)(2,1)}, bf16[4,1024,128]{2,1,0:T(8,128)(2,1)}, u32[]{:S(2)}, u32[]{:S(2)}) collective-permute-start(bf16[4,1024,128]{2,1,0:T(8,128)(2,1)} %collective-permute-done.7.refs_5_.refs_1_), channel_id=1, source_target_pairs={{0,1},{1,2},{2,3},{3,0},{4,5},{5,6},{6,7},{7,4},{8,11},{9,8},{10,9... | collective-permute-start | bytes 3145736 | tf_op jit(solution)/shard_map/ppermute | solution.py:210
  71.4 0.1 stack.95.place_ref
  71.4 9.5 %shard_map.28.refs_16_ = bf16[1024,2048]{1,0:T(8,128)(2,1)} custom-call(s32[8]{0:T(128)S(1)} %stack.95.place_ref, bf16[4,1024,128]{2,1,0:T(8,128)(2,1)S(1)} %pad_maximum_fusion.refs_0_, bf16[4,1024,128]{2,1,0:T(8,128)(2,1)S(1)} %collective-permute-done.15.refs_1_, bf16[4,1024,128]{2,1,0:T(8,128)(2,1)S(1)} %collective-permute-done.16.refs_2_, ...), custom_call_target="tpu_custom_call" | custom-call | flops 42949672 | bytes 209715 | tf_op jit(solution)/shard_map/pallas_call | solution.py:143
  80.9 0.5 collective-permute-done.24.refs_13_
  81.4 2.1 %collective-permute-start.25 = (bf16[1,256,2048]{2,1,0:T(8,128)(2,1)}, bf16[1,256,2048]{2,1,0:T(8,128)(2,1)}, u32[]{:S(2)}, u32[]{:S(2)}) collective-permute-start(bf16[1,256,2048]{2,1,0:T(8,128)(2,1)} %collective-permute-done.24.refs_13_), channel_id=1, source_target_pairs={{0,8},{1,9},{2,10},{3,11},{4,12},{5,13},{6,14},{7,15},{8,0},{9,1},... | collective-permute-start | bytes 3145736 | tf_op jit(solution)/shard_map/ppermute | solution.py:210
  83.5 0.0 collective-permute-done.11.refs_4_
  83.5 0.0 collective-permute-start.22
  83.5 3.2 %collective-permute-done.17.refs_5_ = bf16[1,256,2048]{2,1,0:T(8,128)(2,1)} collective-permute-done((bf16[1,256,2048]{2,1,0:T(8,128)(2,1)}, bf16[1,256,2048]{2,1,0:T(8,128)(2,1)}, u32[]{:S(2)}, u32[]{:S(2)}) %collective-permute-start.17) | collective-permute-done | bytes 1048608 | tf_op jit(solution)/shard_map/ppermute | solution.py:210
  86.7 4.9 %collective-permute-start.23 = (bf16[1,256,2048]{2,1,0:T(8,128)(2,1)}, bf16[1,256,2048]{2,1,0:T(8,128)(2,1)}, u32[]{:S(2)}, u32[]{:S(2)}) collective-permute-start(bf16[1,256,2048]{2,1,0:T(8,128)(2,1)} %collective-permute-done.14.refs_9_), channel_id=1, source_target_pairs={{0,8},{1,9},{2,10},{3,11},{4,12},{5,13},{6,14},{7,15},{8,0},{9,1},... | collective-permute-start | bytes 3145736 | tf_op jit(solution)/shard_map/ppermute | solution.py:210
  91.6 0.0 collective-permute-done.9.refs_7_.refs_3_
  91.6 1.0 collective-permute-start.18
  92.7 0.8 collective-permute-done.8.refs_6_.refs_2_
  93.5 0.0 collective-permute-start.19
  93.5 0.1 stack.112.place_ref
  93.6 0.0 collective-permute-done.25.refs_15_
  93.6 0.0 collective-permute-done.22.refs_10_
  93.6 0.6 collective-permute-done.23.refs_11_
  94.2 15.2 %shard_map.29.refs_8_ = bf16[1024,2048]{1,0:T(8,128)(2,1)} custom-call(s32[16]{0:T(128)S(1)} %stack.112.place_ref, bf16[4,1024,128]{2,1,0:T(8,128)(2,1)S(1)} %pad_maximum_fusion.refs_0_, bf16[4,1024,128]{2,1,0:T(8,128)(2,1)S(1)} %collective-permute-done.15.refs_1_, bf16[4,1024,128]{2,1,0:T(8,128)(2,1)S(1)} %collective-permute-done.16.refs_2_, ...), custom_call_target="tpu_custom_call" | custom-call | flops 8589934592 | bytes 20971520 | tf_op jit(solution)/shard_map/pallas_call | solution.py:143
  109.5 0.0 collective-permute-done.18.refs_6_
  109.5 0.0 collective-permute-done.19.refs_7_
  109.5 10.7 %shard_map.30 = bf16[1024,2048]{1,0:T(8,128)(2,1)} custom-call(s32[8]{0:T(128)S(1)} %stack.95.place_ref, bf16[4,1024,128]{2,1,0:T(8,128)(2,1)} %constant_dynamic-update-slice_fusion.refs_4_.refs_0_, bf16[4,1024,128]{2,1,0:T(8,128)(2,1)} %collective-permute-done.7.refs_5_.refs_1_, bf16[4,1024,128]{2,1,0:T(8,128)(2,1)} %collective-permute-done.8.refs_6_.refs_2_, ...), custom_call_target="tpu_custom_call" | custom-call | flops 12884901888 | bytes 62914560 | tf_op jit(solution)/shard_map/pallas_call | solution.py:143
  (8 shorter events, 0.0 us)
Async XLA Ops:
  1.3 7.6 %collective-permute-start = (bf16[1,1024,128]{2,1,0:T(8,128)(2,1)S(1)}, bf16[1,1024,128]{2,1,0:T(8,128)(2,1)S(1)}, u32[]{:S(2)}, u32[]{:S(2)}) collective-permute-start(bf16[1,1024,128]{2,1,0:T(8,128)(2,1)S(1)} %get-tuple-element.26), channel_id=1, source_target_pairs={{0,4},{1,5},{2,6},{3,7},{4,0},{5,1},{6,2},{7,3},{8,12},{9,13},{10,... | collective-permute-start | bytes 786440 | tf_op jit(solution)/shard_map/ppermute | solution.py:210
  3.4 9.1 %collective-permute-start.2 = (bf16[1,1024,128]{2,1,0:T(8,128)(2,1)S(1)}, bf16[1,1024,128]{2,1,0:T(8,128)(2,1)S(1)}, u32[]{:S(2)}, u32[]{:S(2)}) collective-permute-start(bf16[1,1024,128]{2,1,0:T(8,128)(2,1)S(1)} %get-tuple-element.25), channel_id=1, source_target_pairs={{0,32},{1,33},{2,34},{3,35},{4,36},{5,37},{6,38},{7,39},{8,104},{9... | collective-permute-start | bytes 786440 | tf_op jit(solution)/shard_map/ppermute | solution.py:210
  6.1 8.2 %collective-permute-start.3 = (bf16[1,1024,128]{2,1,0:T(8,128)(2,1)S(1)}, bf16[1,1024,128]{2,1,0:T(8,128)(2,1)S(1)}, u32[]{:S(2)}, u32[]{:S(2)}) collective-permute-start(bf16[1,1024,128]{2,1,0:T(8,128)(2,1)S(1)} %get-tuple-element.28), channel_id=1, source_target_pairs={{0,96},{1,97},{2,98},{3,99},{4,100},{5,101},{6,102},{7,103},{8,40}... | collective-permute-start | bytes 786440 | tf_op jit(solution)/shard_map/ppermute | solution.py:210
  6.1 25.5 %collective-permute-start.5 = (bf16[1,256,2048]{2,1,0:T(8,128)(2,1)}, bf16[1,256,2048]{2,1,0:T(8,128)(2,1)}, u32[]{:S(2)}, u32[]{:S(2)}) collective-permute-start(bf16[1,256,2048]{2,1,0:T(8,128)(2,1)} %bitcast.12.refs_4_), channel_id=1, source_target_pairs={{0,96},{1,97},{2,98},{3,99},{4,100},{5,101},{6,102},{7,103},{8,40}... | collective-permute-start | bytes 3145736 | tf_op jit(solution)/shard_map/ppermute | solution.py:210
  6.1 27.4 %collective-permute-start.12 = (bf16[1,256,2048]{2,1,0:T(8,128)(2,1)}, bf16[1,256,2048]{2,1,0:T(8,128)(2,1)S(1)}, u32[]{:S(2)}, u32[]{:S(2)}) collective-permute-start(bf16[1,256,2048]{2,1,0:T(8,128)(2,1)} %bitcast.12.refs_4_), channel_id=1, source_target_pairs={{0,16},{1,17},{2,18},{3,19},{4,20},{5,21},{6,22},{7,23},{8,24},{9,... | collective-permute-start | bytes 3145736 | tf_op jit(solution)/shard_map/ppermute | solution.py:210
  8.9 22.6 %collective-permute-start.1 = (bf16[1,1024,128]{2,1,0:T(8,128)(2,1)S(1)}, bf16[1,1024,128]{2,1,0:T(8,128)(2,1)S(1)}, u32[]{:S(2)}, u32[]{:S(2)}) collective-permute-start(bf16[1,1024,128]{2,1,0:T(8,128)(2,1)S(1)} %get-tuple-element.15), channel_id=1, source_target_pairs={{0,64},{1,65},{2,66},{3,67},{4,68},{5,69},{6,70},{7,71},{8,72},{9,... | collective-permute-start | bytes 786440 | tf_op jit(solution)/shard_map/ppermute | solution.py:210
  14.5 26.5 %collective-permute-start.15 = (bf16[4,1024,128]{2,1,0:T(8,128)(2,1)S(1)}, bf16[4,1024,128]{2,1,0:T(8,128)(2,1)S(1)}, u32[]{:S(2)}, u32[]{:S(2)}) collective-permute-start(bf16[4,1024,128]{2,1,0:T(8,128)(2,1)S(1)} %pad_maximum_fusion.refs_0_), channel_id=1, source_target_pairs={{0,1},{1,2},{2,3},{3,0},{4,5},{5,6},{6,7},{7,4},{8,11},{9,8},{10,9... | collective-permute-start | bytes 3145736 | tf_op jit(solution)/shard_map/ppermute | solution.py:210
  18.3 26.1 %collective-permute-start.13 = (bf16[4,1024,128]{2,1,0:T(8,128)(2,1)S(1)}, bf16[4,1024,128]{2,1,0:T(8,128)(2,1)S(1)}, u32[]{:S(2)}, u32[]{:S(2)}) collective-permute-start(bf16[4,1024,128]{2,1,0:T(8,128)(2,1)S(1)} %pad_maximum_fusion.refs_0_), channel_id=1, source_target_pairs={{0,3},{1,0},{2,1},{3,2},{4,7},{5,4},{6,5},{7,6},{8,9},{9,10},{10,1... | collective-permute-start | bytes 3145736 | tf_op jit(solution)/shard_map/ppermute | solution.py:210
  31.6 18.1 %collective-permute-start.4 = (bf16[3,1024,128]{2,1,0:T(8,128)(2,1)S(1)}, bf16[3,1024,128]{2,1,0:T(8,128)(2,1)S(1)}, u32[]{:S(2)}, u32[]{:S(2)}) collective-permute-start(bf16[3,1024,128]{2,1,0:T(8,128)(2,1)S(1)} %pad_maximum_fusion.1), channel_id=1, source_target_pairs={{0,4},{1,5},{2,6},{3,7},{4,0},{5,1},{6,2},{7,3},{8,12},{9,13},{10,... | collective-permute-start | bytes 2359304 | tf_op jit(solution)/shard_map/ppermute | solution.py:210
  31.7 19.7 %collective-permute-start.6 = (bf16[1,256,2048]{2,1,0:T(8,128)(2,1)}, bf16[1,256,2048]{2,1,0:T(8,128)(2,1)S(1)}, u32[]{:S(2)}, u32[]{:S(2)}) collective-permute-start(bf16[1,256,2048]{2,1,0:T(8,128)(2,1)} %collective-permute-done.5.refs_12_), channel_id=1, source_target_pairs={{0,8},{1,9},{2,10},{3,11},{4,12},{5,13},{6,14},{7,15},{8,0},{9,1},... | collective-permute-start | bytes 3145736 | tf_op jit(solution)/shard_map/ppermute | solution.py:210
  33.5 25.1 %copy-start.1 = (bf16[1,256,2048]{2,1,0:T(8,128)(2,1)}, bf16[1,256,2048]{2,1,0:T(8,128)(2,1)S(1)}, u32[]{:S(2)}) copy-start(bf16[1,256,2048]{2,1,0:T(8,128)(2,1)S(1)} %collective-permute-done.12.refs_5_) | copy-start | bytes 3145732
  33.5 18.4 %collective-permute-start.10 = (bf16[1,256,2048]{2,1,0:T(8,128)(2,1)}, bf16[1,256,2048]{2,1,0:T(8,128)(2,1)}, u32[]{:S(2)}, u32[]{:S(2)}) collective-permute-start(bf16[1,256,2048]{2,1,0:T(8,128)(2,1)} %bitcast.12.refs_4_), channel_id=1, source_target_pairs={{0,32},{1,33},{2,34},{3,35},{4,36},{5,37},{6,38},{7,39},{8,104},{9... | collective-permute-start | bytes 3145736 | tf_op jit(solution)/shard_map/ppermute | solution.py:210
  41.0 15.2 %collective-permute-start.16 = (bf16[4,1024,128]{2,1,0:T(8,128)(2,1)S(1)}, bf16[4,1024,128]{2,1,0:T(8,128)(2,1)S(1)}, u32[]{:S(2)}, u32[]{:S(2)}) collective-permute-start(bf16[4,1024,128]{2,1,0:T(8,128)(2,1)S(1)} %collective-permute-done.15.refs_1_), channel_id=1, source_target_pairs={{0,1},{1,2},{2,3},{3,0},{4,5},{5,6},{6,7},{7,4},{8,11},{9,8},{10,9... | collective-permute-start | bytes 3145736 | tf_op jit(solution)/shard_map/ppermute | solution.py:210
  44.4 11.7 %copy-start = (bf16[4,1024,128]{2,1,0:T(8,128)(2,1)}, bf16[4,1024,128]{2,1,0:T(8,128)(2,1)S(1)}, u32[]{:S(2)}) copy-start(bf16[4,1024,128]{2,1,0:T(8,128)(2,1)S(1)} %collective-permute-done.13.refs_3_) | copy-start | bytes 3145732
  44.4 15.6 %collective-permute-start.14 = (bf16[1,256,2048]{2,1,0:T(8,128)(2,1)S(1)}, bf16[1,256,2048]{2,1,0:T(8,128)(2,1)}, u32[]{:S(2)}, u32[]{:S(2)}) collective-permute-start(bf16[1,256,2048]{2,1,0:T(8,128)(2,1)S(1)} %collective-permute-done.12.refs_5_), channel_id=1, source_target_pairs={{0,32},{1,33},{2,34},{3,35},{4,36},{5,37},{6,38},{7,39},{8,104},{9... | collective-permute-start | bytes 3145736 | tf_op jit(solution)/shard_map/ppermute | solution.py:210
  49.7 13.8 %collective-permute-start.20 = (bf16[1,256,2048]{2,1,0:T(8,128)(2,1)}, bf16[1,256,2048]{2,1,0:T(8,128)(2,1)S(1)}, u32[]{:S(2)}, u32[]{:S(2)}) collective-permute-start(bf16[1,256,2048]{2,1,0:T(8,128)(2,1)} %bitcast.12.refs_4_), channel_id=1, source_target_pairs={{0,8},{1,9},{2,10},{3,11},{4,12},{5,13},{6,14},{7,15},{8,0},{9,1},... | collective-permute-start | bytes 3145736 | tf_op jit(solution)/shard_map/ppermute | solution.py:210
  51.4 16.6 %copy-start.4 = (bf16[1,256,2048]{2,1,0:T(8,128)(2,1)}, bf16[1,256,2048]{2,1,0:T(8,128)(2,1)S(1)}, u32[]{:S(2)}) copy-start(bf16[1,256,2048]{2,1,0:T(8,128)(2,1)S(1)} %collective-permute-done.6.refs_14_) | copy-start | bytes 3145732
  51.4 12.2 %collective-permute-start.21 = (bf16[1,256,2048]{2,1,0:T(8,128)(2,1)S(1)}, bf16[1,256,2048]{2,1,0:T(8,128)(2,1)S(1)}, u32[]{:S(2)}, u32[]{:S(2)}) collective-permute-start(bf16[1,256,2048]{2,1,0:T(8,128)(2,1)S(1)} %collective-permute-done.12.refs_5_), channel_id=1, source_target_pairs={{0,8},{1,9},{2,10},{3,11},{4,12},{5,13},{6,14},{7,15},{8,0},{9,1},... | collective-permute-start | bytes 3145736 | tf_op jit(solution)/shard_map/ppermute | solution.py:210
  51.9 16.1 %collective-permute-start.7 = (bf16[4,1024,128]{2,1,0:T(8,128)(2,1)}, bf16[4,1024,128]{2,1,0:T(8,128)(2,1)}, u32[]{:S(2)}, u32[]{:S(2)}) collective-permute-start(bf16[4,1024,128]{2,1,0:T(8,128)(2,1)} %constant_dynamic-update-slice_fusion.refs_4_.refs_0_), channel_id=1, source_target_pairs={{0,1},{1,2},{2,3},{3,0},{4,5},{5,6},{6,7},{7,4},{8,11},{9,8},{10,9... | collective-permute-start | bytes 3145736 | tf_op jit(solution)/shard_map/ppermute | solution.py:210
  56.1 25.3 %collective-permute-start.24 = (bf16[1,256,2048]{2,1,0:T(8,128)(2,1)}, bf16[1,256,2048]{2,1,0:T(8,128)(2,1)}, u32[]{:S(2)}, u32[]{:S(2)}) collective-permute-start(bf16[1,256,2048]{2,1,0:T(8,128)(2,1)} %collective-permute-done.5.refs_12_), channel_id=1, source_target_pairs={{0,16},{1,17},{2,18},{3,19},{4,20},{5,21},{6,22},{7,23},{8,24},{9,... | collective-permute-start | bytes 3145736 | tf_op jit(solution)/shard_map/ppermute | solution.py:210
  59.9 23.6 %collective-permute-start.11 = (bf16[1,256,2048]{2,1,0:T(8,128)(2,1)}, bf16[1,256,2048]{2,1,0:T(8,128)(2,1)}, u32[]{:S(2)}, u32[]{:S(2)}) collective-permute-start(bf16[1,256,2048]{2,1,0:T(8,128)(2,1)} %collective-permute-done.10.refs_8_), channel_id=1, source_target_pairs={{0,32},{1,33},{2,34},{3,35},{4,36},{5,37},{6,38},{7,39},{8,104},{9... | collective-permute-start | bytes 3145736 | tf_op jit(solution)/shard_map/ppermute | solution.py:210
  63.5 1.0 copy-start.2
  63.5 23.3 %collective-permute-start.17 = (bf16[1,256,2048]{2,1,0:T(8,128)(2,1)}, bf16[1,256,2048]{2,1,0:T(8,128)(2,1)}, u32[]{:S(2)}, u32[]{:S(2)}) collective-permute-start(bf16[1,256,2048]{2,1,0:T(8,128)(2,1)} %collective-permute-done.14.refs_9_), channel_id=1, source_target_pairs={{0,32},{1,33},{2,34},{3,35},{4,36},{5,37},{6,38},{7,39},{8,104},{9... | collective-permute-start | bytes 3145736 | tf_op jit(solution)/shard_map/ppermute | solution.py:210
  64.4 1.6 %copy-start.3 = (bf16[1,256,2048]{2,1,0:T(8,128)(2,1)}, bf16[1,256,2048]{2,1,0:T(8,128)(2,1)S(1)}, u32[]{:S(2)}) copy-start(bf16[1,256,2048]{2,1,0:T(8,128)(2,1)S(1)} %collective-permute-done.21.refs_7_) | copy-start | bytes 3145732
  64.4 27.2 %collective-permute-start.9 = (bf16[4,1024,128]{2,1,0:T(8,128)(2,1)}, bf16[4,1024,128]{2,1,0:T(8,128)(2,1)}, u32[]{:S(2)}, u32[]{:S(2)}) collective-permute-start(bf16[4,1024,128]{2,1,0:T(8,128)(2,1)} %constant_dynamic-update-slice_fusion.refs_4_.refs_0_), channel_id=1, source_target_pairs={{0,3},{1,0},{2,1},{3,2},{4,7},{5,4},{6,5},{7,6},{8,9},{9,10},{10,1... | collective-permute-start | bytes 3145736 | tf_op jit(solution)/shard_map/ppermute | solution.py:210
  67.9 25.5 %collective-permute-start.8 = (bf16[4,1024,128]{2,1,0:T(8,128)(2,1)}, bf16[4,1024,128]{2,1,0:T(8,128)(2,1)}, u32[]{:S(2)}, u32[]{:S(2)}) collective-permute-start(bf16[4,1024,128]{2,1,0:T(8,128)(2,1)} %collective-permute-done.7.refs_5_.refs_1_), channel_id=1, source_target_pairs={{0,1},{1,2},{2,3},{3,0},{4,5},{5,6},{6,7},{7,4},{8,11},{9,8},{10,9... | collective-permute-start | bytes 3145736 | tf_op jit(solution)/shard_map/ppermute | solution.py:210
  81.4 12.2 %collective-permute-start.25 = (bf16[1,256,2048]{2,1,0:T(8,128)(2,1)}, bf16[1,256,2048]{2,1,0:T(8,128)(2,1)}, u32[]{:S(2)}, u32[]{:S(2)}) collective-permute-start(bf16[1,256,2048]{2,1,0:T(8,128)(2,1)} %collective-permute-done.24.refs_13_), channel_id=1, source_target_pairs={{0,8},{1,9},{2,10},{3,11},{4,12},{5,13},{6,14},{7,15},{8,0},{9,1},... | collective-permute-start | bytes 3145736 | tf_op jit(solution)/shard_map/ppermute | solution.py:210
  83.5 10.1 %collective-permute-start.22 = (bf16[1,256,2048]{2,1,0:T(8,128)(2,1)}, bf16[1,256,2048]{2,1,0:T(8,128)(2,1)}, u32[]{:S(2)}, u32[]{:S(2)}) collective-permute-start(bf16[1,256,2048]{2,1,0:T(8,128)(2,1)} %collective-permute-done.10.refs_8_), channel_id=1, source_target_pairs={{0,8},{1,9},{2,10},{3,11},{4,12},{5,13},{6,14},{7,15},{8,0},{9,1},... | collective-permute-start | bytes 3145736 | tf_op jit(solution)/shard_map/ppermute | solution.py:210
  86.7 7.5 %collective-permute-start.23 = (bf16[1,256,2048]{2,1,0:T(8,128)(2,1)}, bf16[1,256,2048]{2,1,0:T(8,128)(2,1)}, u32[]{:S(2)}, u32[]{:S(2)}) collective-permute-start(bf16[1,256,2048]{2,1,0:T(8,128)(2,1)} %collective-permute-done.14.refs_9_), channel_id=1, source_target_pairs={{0,8},{1,9},{2,10},{3,11},{4,12},{5,13},{6,14},{7,15},{8,0},{9,1},... | collective-permute-start | bytes 3145736 | tf_op jit(solution)/shard_map/ppermute | solution.py:210
  91.6 17.9 %collective-permute-start.18 = (bf16[1,256,2048]{2,1,0:T(8,128)(2,1)}, bf16[1,256,2048]{2,1,0:T(8,128)(2,1)}, u32[]{:S(2)}, u32[]{:S(2)}) collective-permute-start(bf16[1,256,2048]{2,1,0:T(8,128)(2,1)} %collective-permute-done.11.refs_4_), channel_id=1, source_target_pairs={{0,8},{1,9},{2,10},{3,11},{4,12},{5,13},{6,14},{7,15},{8,0},{9,1},... | collective-permute-start | bytes 3145736 | tf_op jit(solution)/shard_map/ppermute | solution.py:210
  93.5 16.0 %collective-permute-start.19 = (bf16[1,256,2048]{2,1,0:T(8,128)(2,1)}, bf16[1,256,2048]{2,1,0:T(8,128)(2,1)}, u32[]{:S(2)}, u32[]{:S(2)}) collective-permute-start(bf16[1,256,2048]{2,1,0:T(8,128)(2,1)} %collective-permute-done.17.refs_5_), channel_id=1, source_target_pairs={{0,8},{1,9},{2,10},{3,11},{4,12},{5,13},{6,14},{7,15},{8,0},{9,1},... | collective-permute-start | bytes 3145736 | tf_op jit(solution)/shard_map/ppermute | solution.py:210
